TPU v7x, 256 devices: a whole 4x4x8 slice. The times are simulated.
256 devices in a mesh: row: 64 (over x, z, core), col: 4 (over y).
Axes of the slice: x: 4, y: 4, z: 8, core: 2. Of those that a mesh axis runs over, the one named last changes fastest.
Arguments:
- factor: bfloat16 [64, 16, 4, 256, 256], P('row', None, 'col'), may hold values from -0.09375 to 0.09375
- diag_inverse: bfloat16 [64, 256, 256], P('row'), may hold values from -2 to 2, as said below
- right_side: bfloat16 [64, 64, 256], P('row'), may hold values from -6 to 6
- levels: int32 [64], replicated, may hold values from 0 to 3
- pattern: int32 [64, 16, 4], P('row', None, 'col'), may hold values 0 or 1
Outputs:
- forward: bfloat16 [64, 64, 256], P('row')
- solution: bfloat16 [64, 64, 256], P('row')
Inputs may be any that keep to these rules, and one draw needn't show every extreme that they name: `diag_inverse`: each block is the inverse of a factor diagonal block, nonsingular.
All inputs are finite; a program needn't handle non-finite values. No bound on the sum of `pattern` on one device may be relied on, other than what follows from the above.
Results may differ from a plain program's by a relative error of at most 0.014.
Values may be sent and summed in bfloat16 or wider, within the bound.
No kernel may reach another device: no remote copies, remote signals or barrier semaphores. Data moves between devices by JAX's collectives and lax.ppermute only.
A program may use at most 64 MiB of HBM per device.

v0:
```python
import functools

import jax
import jax.numpy as jnp
from jax import lax
from jax.experimental import pallas as pl
from jax.experimental.pallas import tpu as pltpu
from jax.sharding import Mesh, PartitionSpec as P

LEVELS = 4
NX, NZ, NK, NY = 4, 8, 2, 4
HZ = NZ // 2
F32, BF16 = jnp.float32, jnp.bfloat16
HELD = 20
BOUNDS = 2 * NX * HZ + 1
ROWS = BOUNDS + 2 * LEVELS + 1


def pairs(n, bits):
    return [(i, i ^ bits) for i in range(n)]


def swap(v):
    return lax.ppermute(v, "k", [(0, 1), (1, 0)])


def times_transposed(v, d):
    return lax.dot_general(v, d, (((1,), (1,)), ((), ())), preferred_element_type=F32)


def fetch_all(moves, sems):
    copies = [pltpu.make_async_copy(source, to, sems.at[i]) for i, (source, to) in enumerate(moves)]
    for copy in copies:
        copy.start()
    for copy in copies:
        copy.wait()


def first_rows(levels_hbm, b_hbm, d_hbm, row_levels, b_own, f_own, levels, d, sems):
    x, z, k = (lax.axis_index(a) for a in ("x", "z", "k"))
    own = (x * NZ + z) * NK + k
    half = b_own.shape[0]
    b_mine = b_hbm.at[pl.ds(pl.multiple_of(k * half, half), half), :]
    fetch_all(((levels_hbm, levels), (b_mine, b_own), (d_hbm, d)), sems)
    level = levels[own]
    row_levels[0] = jnp.full(row_levels.shape[1:], level, jnp.int32)
    row_levels[1] = jnp.full(row_levels.shape[1:], levels[own + 1 - 2 * k], jnp.int32)
    f_own[...] = jnp.where(level == 0, times_transposed(b_own[...], d[...]), 0.0).astype(BF16)


def make_plan(levels, patterns, plan):
    x, z, k, y = (lax.axis_index(a) for a in ("x", "z", "k", "y"))
    own = (x * NZ + z) * NK + k
    used = jnp.int32(0)
    for r, row in enumerate((own, own + 1 - 2 * k)):
        row_level = levels[row]
        plan[ROWS + r] = row_level
        cols = []
        for s in range(NX):
            first = (x ^ s) * HZ
            for i in range(HZ):
                level = levels[(first + i) * NY + y]
                usable = (patterns[r][first + i] == 1) & (level < row_level)
                cols.append(jnp.where(usable, level, LEVELS))
        for level in range(LEVELS):
            plan[BOUNDS + r * LEVELS + level] = used
            if level < LEVELS - 1:
                for n, col in enumerate(cols):
                    plan[used] = r * NX * HZ + n
                    used = used + jnp.where(col == level, 1, 0)
    plan[BOUNDS + 2 * LEVELS] = used


def block_column(x, n):
    return (x ^ (n // HZ)) * HZ + n % HZ


def prepare(levels_hbm, pattern_hbm, pattern_par, l_own, l_par, here, plan, held, rest, passed, levels, pattern_own, sems):
    passed[...] = here[...]
    fetch_all(((levels_hbm, levels), (pattern_hbm, pattern_own)), sems)
    make_plan(levels, (pattern_own, pattern_par), plan)
    x = lax.axis_index("x")

    def each(then):
        def step(place, carry):
            n = plan[place]
            j = block_column(x, n % (NX * HZ))
            for r, blocks in enumerate((l_own, l_par)):
                mine = n // (NX * HZ) == r

                @pl.when(mine & (place < HELD))
                def _():
                    to = held.at[jnp.minimum(place, HELD - 1)]
                    then(pltpu.make_async_copy(blocks.at[j], to, sems.at[place]))

                @pl.when(mine & (place >= HELD))
                def _():
                    to = rest.at[jnp.maximum(place - HELD, 0)]
                    then(pltpu.make_async_copy(blocks.at[j], to, sems.at[place]))

            return carry

        lax.fori_loop(0, plan[BOUNDS + 2 * LEVELS], step, 0)

    each(lambda copy: copy.start())
    each(lambda copy: copy.wait())


def use_blocks(plan, r, first, last, held, rest, spare, sem, use):
    def step(place, carry):
        n = plan[place] - r * NX * HZ

        @pl.when(place < HELD)
        def _():
            use(n, held[jnp.minimum(place, HELD - 1)])

        @pl.when(place >= HELD)
        def _():
            copy = pltpu.make_async_copy(rest.at[jnp.maximum(place - HELD, 0)], spare, sem)
            copy.start()
            copy.wait()
            use(n, spare[...])

        return carry

    lax.fori_loop(first, last, step, 0)


def forward_products(level, plan, arrived, held, rest, p_in, p_out, sent, spare, sem):
    p_out[...] = p_in[...]
    for r in range(2):

        def use(n, block, r=r):
            p_out[r] += times_transposed(arrived[n], block)

        at = BOUNDS + r * LEVELS + level - 1
        use_blocks(plan, r, plan[at], plan[at + 1], held, rest, spare, sem, use)
    k = lax.axis_index("k")
    sent[0] = jnp.where(k == 0, p_out[0], p_out[1]).astype(BF16)
    sent[1] = jnp.where(k == 0, p_out[1], p_out[0]).astype(BF16)


def backward_products(level, plan, o_own, o_par, held, rest, t0, t1, t2, t3, total, spare, sem):
    total[...] = jnp.zeros_like(total)
    for r, solved in enumerate((o_own, o_par)):

        def use(n, block, solved=solved):
            total[n] += jnp.dot(solved[...], block, preferred_element_type=F32)

        @pl.when(plan[ROWS + r] == level + 1)
        def _(r=r, use=use):
            at = BOUNDS + r * LEVELS
            use_blocks(plan, r, plan[at], plan[at + LEVELS], held, rest, spare, sem, use)

    t0[...] = total[0:HZ]
    for s, out in ((1, t1), (2, t2), (3, t3)):
        out[...] = total[s * HZ : (s + 1) * HZ].astype(BF16)


def in_hbm(v):
    return pltpu.with_memory_space_constraint(v, pltpu.HBM)


def shards(factor, diag_inverse, right_side, levels, pattern):
    n_j, width = factor.shape[1], factor.shape[3]
    n_rhs = right_side.shape[1]
    half = n_rhs // NK
    x, z, k, y = (lax.axis_index(a) for a in ("x", "z", "k", "y"))
    is_own = k == y % 2

    d_own = diag_inverse[0]
    d_par = swap(d_own)
    b_par = swap(right_side[0])
    pattern_own = pattern.reshape(n_j)
    pattern_par = swap(pattern_own)
    vmem, smem = pl.BlockSpec(memory_space=pltpu.VMEM), pl.BlockSpec(memory_space=pltpu.SMEM)
    anywhere = pl.BlockSpec(memory_space=pl.ANY)
    params = pltpu.CompilerParams(vmem_limit_bytes=2 << 20)
    row_levels, b_own, f_own = pl.pallas_call(
        first_rows,
        in_specs=[anywhere] * 3,
        out_specs=[vmem] * 3,
        out_shape=[
            jax.ShapeDtypeStruct((2, half, width), jnp.int32),
            jax.ShapeDtypeStruct((half, width), BF16),
            jax.ShapeDtypeStruct((half, width), BF16),
        ],
        scratch_shapes=[
            pltpu.SMEM(levels.shape, jnp.int32),
            pltpu.VMEM((width, width), BF16),
            pltpu.SemaphoreType.DMA((3,)),
        ],
        compiler_params=params,
    )(in_hbm(levels), in_hbm(right_side[0]), in_hbm(d_own))
    l_own = factor.reshape(n_j, width, width)
    l_own, d_par, b_par, pattern_par, row_levels = lax.optimization_barrier((l_own, d_par, b_par, pattern_par, row_levels))
    l_par = in_hbm(swap(l_own))
    l_own = in_hbm(l_own)
    level_own, level_par = row_levels[0], row_levels[1]
    b_par = lax.dynamic_slice_in_dim(b_par, k * half, half, 0)

    def solve(v, d):
        return jnp.einsum("kb,ab->ka", v.astype(BF16), d, preferred_element_type=F32).astype(BF16)

    def solve_t(v, d):
        return jnp.einsum("ka,ab->kb", v.astype(BF16), d, preferred_element_type=F32).astype(BF16)

    zero = jnp.zeros((half, width), BF16)
    f_par = jnp.where(level_par == 0, solve(b_par, d_par), zero)
    b_own, b_par = b_own.astype(F32), b_par.astype(F32)

    fetch = [pltpu.VMEM((width, width), BF16), pltpu.SemaphoreType.DMA]
    products = [jax.ShapeDtypeStruct((2, half, width), t) for t in (F32, BF16)]
    level_r = jnp.where(is_own, level_own, level_par)
    sums = jnp.zeros((2, half, width), F32)
    for level in range(1, LEVELS):
        f_r = jnp.where(is_own, f_own, f_par)
        sent = jnp.where(level_r == level - 1, f_r, zero)
        got = lax.all_to_all(jnp.broadcast_to(sent[None], (NZ, half, width)), "z", 0, 0)
        got = lax.dynamic_index_in_dim(got.reshape(HZ, 2, half, width), y // 2, 1, keepdims=False)
        parts = [got] + [lax.ppermute(got, "x", pairs(NX, s)) for s in (1, 2, 3)]
        if level == 1:
            plan, held, rest, got = pl.pallas_call(
                prepare,
                in_specs=[anywhere] * 2 + [smem] + [anywhere] * 2 + [vmem],
                out_specs=[smem, vmem, anywhere, vmem],
                out_shape=[
                    pltpu.SMEM((ROWS + 2,), jnp.int32),
                    pltpu.VMEM((HELD, width, width), BF16),
                    pltpu.HBM((2 * n_j - HELD, width, width), BF16),
                    jax.ShapeDtypeStruct((HZ, half, width), BF16),
                ],
                scratch_shapes=[
                    pltpu.SMEM(levels.shape, jnp.int32),
                    pltpu.SMEM((n_j,), jnp.int32),
                    pltpu.SemaphoreType.DMA((2 * n_j,)),
                ],
                compiler_params=params,

            )(in_hbm(levels), in_hbm(pattern_own), pattern_par, l_own, l_par, got)
            parts[0] = got
            plan = pltpu.with_memory_space_constraint(plan, pltpu.SMEM)
            held = pltpu.with_memory_space_constraint(held, pltpu.VMEM)
            rest = pltpu.with_memory_space_constraint(rest, pltpu.HBM)
        sums, rows = pl.pallas_call(
            functools.partial(forward_products, level),
            in_specs=[smem] + [vmem] * 2 + [anywhere, vmem],
            out_specs=[vmem] * 2,
            out_shape=products,
            scratch_shapes=fetch,
            compiler_params=params,
        )(plan, jnp.concatenate(parts), held, rest, sums)
        others = [lax.ppermute(rows, "y", pairs(NY, s)).astype(F32) for s in (1, 2, 3)]
        other = others[0] + others[1] + others[2]
        s_own = sums[0] + jnp.where(k == 0, other[0], other[1])
        s_par = sums[1] + jnp.where(k == 0, other[1], other[0])
        f_own = jnp.where(level_own == level, solve(b_own - s_own, d_own), f_own)
        f_par = jnp.where(level_par == level, solve(b_par - s_par, d_par), f_par)

    top = LEVELS - 1
    o_own = jnp.where(level_own == top, solve_t(f_own, d_own), zero)
    o_par = jnp.where(level_par == top, solve_t(f_par, d_par), zero)
    f_r = jnp.where(is_own, f_own, f_par)
    d_r = jnp.where(is_own, d_own, d_par)
    o_own, o_par, f_r, d_r = lax.optimization_barrier((o_own, o_par, f_r, d_r))
    r_sum = jnp.zeros((half, width), F32)
    for level in range(top - 1, -1, -1):
        mine, *parts = pl.pallas_call(
            functools.partial(backward_products, level),
            in_specs=[smem] + [vmem] * 3 + [anywhere],
            out_specs=[vmem] * 4,
            out_shape=[jax.ShapeDtypeStruct((HZ, half, width), t) for t in (F32, BF16, BF16, BF16)],
            scratch_shapes=[pltpu.VMEM((n_j, half, width), F32)] + fetch,
            compiler_params=params,
        )(plan, o_own, o_par, held, rest)
        for s in (1, 2, 3):
            mine = mine + lax.ppermute(parts[s - 1], "x", pairs(NX, s)).astype(F32)
        out = jnp.broadcast_to(mine.astype(BF16)[:, None], (HZ, 2, half, width)).reshape(NZ, half, width)
        arrived = lax.all_to_all(out, "z", 0, 0)
        r_sum = r_sum + jnp.sum(arrived.astype(F32), axis=0)
        o_r = solve_t(f_r.astype(F32) - r_sum, d_r)
        got = jnp.stack([o_r] + [lax.ppermute(o_r, "y", pairs(NY, s)) for s in (1, 2, 3)])
        new_own = lax.dynamic_index_in_dim(got, y ^ (2 * (z % 2) + k), 0, keepdims=False)
        new_par = lax.dynamic_index_in_dim(got, y ^ (2 * (z % 2) + 1 - k), 0, keepdims=False)
        o_own = jnp.where(level_own == level, new_own, o_own)
        o_par = jnp.where(level_par == level, new_par, o_par)

    theirs = swap(jnp.stack([f_par, o_par]))
    mine = jnp.stack([f_own, o_own])
    both = jnp.concatenate([jnp.where(k == 0, mine, theirs), jnp.where(k == 0, theirs, mine)], axis=1)
    return (both[0][None], both[1][None])


def solution(mesh):
    fine = Mesh(mesh.devices.reshape(NX, NZ, NK, NY), ("x", "z", "k", "y"))
    row = ("x", "z", "k")
    return jax.shard_map(
        shards,
        mesh=fine,
        in_specs=(
            P(row, None, "y", None, None),
            P(row, None, None),
            P(row, None, None),
            P(),
            P(row, None, "y"),
        ),
        out_specs=(P(row, None, None), P(row, None, None)),
        check_vma=False,
    )
```

profile of v0, /device:TPU:1, one launch (start us, length us, event | category | flops | bytes accessed | tf_op | source)
XLA Modules:
  0.0 177.6 jit_solution(3824141751231227622)
XLA Ops:
  0.6 3.3 %collective-permute-start = (bf16[256,256]{1,0:T(8,128)(2,1)}, bf16[256,256]{1,0:T(8,128)(2,1)S(1)}, u32[]{:S(2)}, u32[]{:S(2)}) collective-permute-start(bf16[256,256]{1,0:T(8,128)(2,1)} %bitcast.128), channel_id=1, source_target_pairs={{0,4},{4,0},{1,5},{5,1},{2,6},{6,2},{3,7},{7,3},{8,12},{12,8},{9,1... | collective-permute-start | bytes 393224 | tf_op jit(solution)/shard_map/ppermute | solution.py:24
  6.7 6.5 %all-to-all-start = ((bf16[8,32,256]{2,1,0:T(8,128)(2,1)}), bf16[8,32,256]{2,1,0:T(8,128)(2,1)S(1)}, u32[]{:S(2)}, u32[]{:S(2)}) async-start(bf16[8,32,256]{2,1,0:T(8,128)(2,1)} %broadcast_in_dim.17), calls=%async_computation | async-start | bytes 262144 | tf_op jit(solution)/shard_map/all_to_all | solution.py:219
  13.2 7.8 %all-to-all-done = bf16[8,32,256]{2,1,0:T(8,128)(2,1)S(1)} async-done(((bf16[8,32,256]{2,1,0:T(8,128)(2,1)}), bf16[8,32,256]{2,1,0:T(8,128)(2,1)S(1)}, u32[]{:S(2)}, u32[]{:S(2)}) %all-to-all-start) | async-done | bytes 131104 | tf_op jit(solution)/shard_map/all_to_all | solution.py:219
  21.0 2.5 %collective-permute-start.6 = (bf16[4,32,256]{2,1,0:T(8,128)(2,1)S(1)}, bf16[4,32,256]{2,1,0:T(8,128)(2,1)S(1)}, u32[]{:S(2)}, u32[]{:S(2)}) collective-permute-start(bf16[4,32,256]{2,1,0:T(8,128)(2,1)S(1)} %dynamic-slice_bitcast_fusion.2.here), channel_id=1, source_target_pairs={{0,192},{64,128},{128,64},{192,0},{1,193},{65,129},{129,65},{193,1... | collective-permute-start | bytes 196616 | tf_op jit(solution)/shard_map/ppermute | solution.py:221
  24.3 2.7 %shard_map.69 = (s32[44]{0:T(128)S(4)}, bf16[20,256,256]{2,1,0:T(8,128)(2,1)S(1)}, bf16[12,256,256]{2,1,0:T(8,128)(2,1)}, bf16[4,32,256]{2,1,0:T(8,128)(2,1)S(1)}) custom-call(s32[64]{0:T(128)} %levels_hbm.3, s32[16]{0:T(128)} %bitcast.155, s32[16]{0:T(128)S(1)} %collective-permute-done.2.pattern_par, bf16[16,256,256]{2,1,0:T(8,128)(2,1)} %bitcast.131, ...), custom_call_target="tpu_custom_call" | custom-call | tf_op jit(solution)/shard_map/pallas_call | solution.py:223
  28.5 2.8 %collective-permute-start.9 = (bf16[2,32,256]{2,1,0:T(8,128)(2,1)S(1)}, bf16[2,32,256]{2,1,0:T(8,128)(2,1)S(1)}, u32[]{:S(2)}, u32[]{:S(2)}) collective-permute-start(bf16[2,32,256]{2,1,0:T(8,128)(2,1)S(1)} %get-tuple-element.49), channel_id=1, source_target_pairs={{0,3},{1,2},{2,1},{3,0},{4,7},{5,6},{6,5},{7,4},{8,11},{9,10},{10,... | collective-permute-start | bytes 98312 | tf_op jit(solution)/shard_map/ppermute | solution.py:253
  32.7 3.0 %collective-permute-done.8 = bf16[2,32,256]{2,1,0:T(8,128)(2,1)S(1)} collective-permute-done((bf16[2,32,256]{2,1,0:T(8,128)(2,1)S(1)}, bf16[2,32,256]{2,1,0:T(8,128)(2,1)S(1)}, u32[]{:S(2)}, u32[]{:S(2)}) %collective-permute-start.8) | collective-permute-done | bytes 32800 | tf_op jit(solution)/shard_map/ppermute | solution.py:253
  36.0 10.3 %all_to_all.30 = bf16[8,32,256]{2,1,0:T(8,128)(2,1)S(1)} all-to-all(bf16[8,32,256]{2,1,0:T(8,128)(2,1)S(1)} %broadcast_in_dim.19), channel_id=1, replica_groups=mesh['x'=4,'z'=8,'k'=2,'y'=4] {'z'}, dimensions={0} | all-to-all | bytes 262144 | tf_op jit(solution)/shard_map/all_to_all | solution.py:219
  46.4 1.6 collective-permute-start.12
  49.6 1.4 collective-permute-done.12
  51.0 1.6 collective-permute-done.11
  52.7 1.7 collective-permute-start.15
  57.0 1.9 %collective-permute-done.14 = bf16[2,32,256]{2,1,0:T(8,128)(2,1)S(1)} collective-permute-done((bf16[2,32,256]{2,1,0:T(8,128)(2,1)S(1)}, bf16[2,32,256]{2,1,0:T(8,128)(2,1)S(1)}, u32[]{:S(2)}, u32[]{:S(2)}) %collective-permute-start.14) | collective-permute-done | bytes 32800 | tf_op jit(solution)/shard_map/ppermute | solution.py:253
  59.3 10.5 %all_to_all.31 = bf16[8,32,256]{2,1,0:T(8,128)(2,1)S(1)} all-to-all(bf16[8,32,256]{2,1,0:T(8,128)(2,1)S(1)} %broadcast_in_dim.20), channel_id=1, replica_groups=mesh['x'=4,'z'=8,'k'=2,'y'=4] {'z'}, dimensions={0} | all-to-all | bytes 262144 | tf_op jit(solution)/shard_map/all_to_all | solution.py:219
  69.9 1.4 collective-permute-start.18
  71.7 1.4 collective-permute-start.16
  74.2 1.7 collective-permute-done.17
  82.1 2.7 %collective-permute-start.24 = (bf16[4,32,256]{2,1,0:T(8,128)(2,1)S(1)}, bf16[4,32,256]{2,1,0:T(8,128)(2,1)S(1)}, u32[]{:S(2)}, u32[]{:S(2)}) collective-permute-start(bf16[4,32,256]{2,1,0:T(8,128)(2,1)S(1)} %get-tuple-element.60), channel_id=1, source_target_pairs={{0,192},{64,128},{128,64},{192,0},{1,193},{65,129},{129,65},{193,1... | collective-permute-start | bytes 196616 | tf_op jit(solution)/shard_map/ppermute | solution.py:277
  85.5 1.4 collective-permute-done.24
  86.9 2.6 %collective-permute-done.23 = bf16[4,32,256]{2,1,0:T(8,128)(2,1)S(1)} collective-permute-done((bf16[4,32,256]{2,1,0:T(8,128)(2,1)S(1)}, bf16[4,32,256]{2,1,0:T(8,128)(2,1)S(1)}, u32[]{:S(2)}, u32[]{:S(2)}) %collective-permute-start.23) | collective-permute-done | bytes 65568 | tf_op jit(solution)/shard_map/ppermute | solution.py:277
  89.5 10.3 %all_to_all.32 = bf16[8,32,256]{2,1,0:T(8,128)(2,1)S(1)} all-to-all(bf16[8,32,256]{2,1,0:T(8,128)(2,1)S(1)} %bitcast.132), channel_id=1, replica_groups=mesh['x'=4,'z'=8,'k'=2,'y'=4] {'z'}, dimensions={0} | all-to-all | bytes 262144 | tf_op jit(solution)/shard_map/all_to_all | solution.py:279
  100.0 1.8 %collective-permute-start.27 = (bf16[32,256]{1,0:T(8,128)(2,1)S(1)}, bf16[32,256]{1,0:T(8,128)(2,1)S(1)}, u32[]{:S(2)}, u32[]{:S(2)}) collective-permute-start(bf16[32,256]{1,0:T(8,128)(2,1)S(1)} %convolution_convert_fusion.2), channel_id=1, source_target_pairs={{0,3},{1,2},{2,1},{3,0},{4,7},{5,6},{6,5},{7,4},{8,11},{9,10},{10,... | collective-permute-start | bytes 49160 | tf_op jit(solution)/shard_map/ppermute | solution.py:282
  103.8 2.1 %collective-permute-done.26 = bf16[32,256]{1,0:T(8,128)(2,1)S(1)} collective-permute-done((bf16[32,256]{1,0:T(8,128)(2,1)S(1)}, bf16[32,256]{1,0:T(8,128)(2,1)S(1)}, u32[]{:S(2)}, u32[]{:S(2)}) %collective-permute-start.26) | collective-permute-done | bytes 16416 | tf_op jit(solution)/shard_map/ppermute | solution.py:282
  108.0 1.3 collective-permute-start.28
  112.1 10.3 %all_to_all.33 = bf16[8,32,256]{2,1,0:T(8,128)(2,1)S(1)} all-to-all(bf16[8,32,256]{2,1,0:T(8,128)(2,1)S(1)} %bitcast.133), channel_id=1, replica_groups=mesh['x'=4,'z'=8,'k'=2,'y'=4] {'z'}, dimensions={0} | all-to-all | bytes 262144 | tf_op jit(solution)/shard_map/all_to_all | solution.py:279
  124.1 1.7 collective-permute-start.31
  127.8 1.7 collective-permute-start.36
  132.2 1.9 %collective-permute-done.35 = bf16[4,32,256]{2,1,0:T(8,128)(2,1)S(1)} collective-permute-done((bf16[4,32,256]{2,1,0:T(8,128)(2,1)S(1)}, bf16[4,32,256]{2,1,0:T(8,128)(2,1)S(1)}, u32[]{:S(2)}, u32[]{:S(2)}) %collective-permute-start.35) | collective-permute-done | bytes 65568 | tf_op jit(solution)/shard_map/ppermute | solution.py:277
  134.2 10.3 %all_to_all.34 = bf16[8,32,256]{2,1,0:T(8,128)(2,1)S(1)} all-to-all(bf16[8,32,256]{2,1,0:T(8,128)(2,1)S(1)} %bitcast.134), channel_id=1, replica_groups=mesh['x'=4,'z'=8,'k'=2,'y'=4] {'z'}, dimensions={0} | all-to-all | bytes 262144 | tf_op jit(solution)/shard_map/all_to_all | solution.py:279
  144.6 1.7 collective-permute-start.39
  148.8 1.6 collective-permute-done.38
  150.5 25.7 %collective-permute-start.40 = (bf16[2,32,256]{2,1,0:T(8,128)(2,1)S(1)}, bf16[2,32,256]{2,1,0:T(8,128)(2,1)S(1)}, u32[]{:S(2)}, u32[]{:S(2)}) collective-permute-start(bf16[2,32,256]{2,1,0:T(8,128)(2,1)S(1)} %pad_maximum_fusion.8), channel_id=1, source_target_pairs={{0,4},{4,0},{1,5},{5,1},{2,6},{6,2},{3,7},{7,3},{8,12},{12,8},{9,1... | collective-permute-start | bytes 98312 | tf_op jit(solution)/shard_map/ppermute | solution.py:24
  (113 shorter events, 37.6 us)
Async XLA Ops:
  0.6 5.0 %collective-permute-start = (bf16[256,256]{1,0:T(8,128)(2,1)}, bf16[256,256]{1,0:T(8,128)(2,1)S(1)}, u32[]{:S(2)}, u32[]{:S(2)}) collective-permute-start(bf16[256,256]{1,0:T(8,128)(2,1)} %bitcast.128), channel_id=1, source_target_pairs={{0,4},{4,0},{1,5},{5,1},{2,6},{6,2},{3,7},{7,3},{8,12},{12,8},{9,1... | collective-permute-start | bytes 393224 | tf_op jit(solution)/shard_map/ppermute | solution.py:24
  5.6 18.6 %collective-permute-start.3 = (bf16[16,256,256]{2,1,0:T(8,128)(2,1)}, bf16[16,256,256]{2,1,0:T(8,128)(2,1)}, u32[]{:S(2)}, u32[]{:S(2)}) collective-permute-start(bf16[16,256,256]{2,1,0:T(8,128)(2,1)} %bitcast.130), channel_id=1, source_target_pairs={{0,4},{4,0},{1,5},{5,1},{2,6},{6,2},{3,7},{7,3},{8,12},{12,8},{9,1... | collective-permute-start | bytes 6291464 | tf_op jit(solution)/shard_map/ppermute | solution.py:24
  6.7 14.3 %all-to-all-start = ((bf16[8,32,256]{2,1,0:T(8,128)(2,1)}), bf16[8,32,256]{2,1,0:T(8,128)(2,1)S(1)}, u32[]{:S(2)}, u32[]{:S(2)}) async-start(bf16[8,32,256]{2,1,0:T(8,128)(2,1)} %broadcast_in_dim.17), calls=%async_computation | async-start | bytes 262144 | tf_op jit(solution)/shard_map/all_to_all | solution.py:219
  21.0 6.0 %collective-permute-start.6 = (bf16[4,32,256]{2,1,0:T(8,128)(2,1)S(1)}, bf16[4,32,256]{2,1,0:T(8,128)(2,1)S(1)}, u32[]{:S(2)}, u32[]{:S(2)}) collective-permute-start(bf16[4,32,256]{2,1,0:T(8,128)(2,1)S(1)} %dynamic-slice_bitcast_fusion.2.here), channel_id=1, source_target_pairs={{0,192},{64,128},{128,64},{192,0},{1,193},{65,129},{129,65},{193,1... | collective-permute-start | bytes 196616 | tf_op jit(solution)/shard_map/ppermute | solution.py:221
  23.5 4.7 %collective-permute-start.5 = (bf16[4,32,256]{2,1,0:T(8,128)(2,1)S(1)}, bf16[4,32,256]{2,1,0:T(8,128)(2,1)S(1)}, u32[]{:S(2)}, u32[]{:S(2)}) collective-permute-start(bf16[4,32,256]{2,1,0:T(8,128)(2,1)S(1)} %dynamic-slice_bitcast_fusion.2.here), channel_id=1, source_target_pairs={{0,128},{64,192},{128,0},{192,64},{1,129},{65,193},{129,1},{193,65... | collective-permute-start | bytes 196616 | tf_op jit(solution)/shard_map/ppermute | solution.py:221
  24.0 4.2 %collective-permute-start.4 = (bf16[4,32,256]{2,1,0:T(8,128)(2,1)S(1)}, bf16[4,32,256]{2,1,0:T(8,128)(2,1)S(1)}, u32[]{:S(2)}, u32[]{:S(2)}) collective-permute-start(bf16[4,32,256]{2,1,0:T(8,128)(2,1)S(1)} %dynamic-slice_bitcast_fusion.2.here), channel_id=1, source_target_pairs={{0,64},{64,0},{128,192},{192,128},{1,65},{65,1},{129,193},{193,129... | collective-permute-start | bytes 196616 | tf_op jit(solution)/shard_map/ppermute | solution.py:221
  28.5 4.1 %collective-permute-start.9 = (bf16[2,32,256]{2,1,0:T(8,128)(2,1)S(1)}, bf16[2,32,256]{2,1,0:T(8,128)(2,1)S(1)}, u32[]{:S(2)}, u32[]{:S(2)}) collective-permute-start(bf16[2,32,256]{2,1,0:T(8,128)(2,1)S(1)} %get-tuple-element.49), channel_id=1, source_target_pairs={{0,3},{1,2},{2,1},{3,0},{4,7},{5,6},{6,5},{7,4},{8,11},{9,10},{10,... | collective-permute-start | bytes 98312 | tf_op jit(solution)/shard_map/ppermute | solution.py:253
  31.4 4.3 %collective-permute-start.8 = (bf16[2,32,256]{2,1,0:T(8,128)(2,1)S(1)}, bf16[2,32,256]{2,1,0:T(8,128)(2,1)S(1)}, u32[]{:S(2)}, u32[]{:S(2)}) collective-permute-start(bf16[2,32,256]{2,1,0:T(8,128)(2,1)S(1)} %get-tuple-element.49), channel_id=1, source_target_pairs={{0,2},{1,3},{2,0},{3,1},{4,6},{5,7},{6,4},{7,5},{8,10},{9,11},{10,... | collective-permute-start | bytes 98312 | tf_op jit(solution)/shard_map/ppermute | solution.py:253
  46.4 4.6 %collective-permute-start.12 = (bf16[4,32,256]{2,1,0:T(8,128)(2,1)S(1)}, bf16[4,32,256]{2,1,0:T(8,128)(2,1)S(1)}, u32[]{:S(2)}, u32[]{:S(2)}) collective-permute-start(bf16[4,32,256]{2,1,0:T(8,128)(2,1)S(1)} %dynamic-slice_bitcast_fusion.1), channel_id=1, source_target_pairs={{0,192},{64,128},{128,64},{192,0},{1,193},{65,129},{129,65},{193,1... | collective-permute-start | bytes 196616 | tf_op jit(solution)/shard_map/ppermute | solution.py:221
  48.0 4.6 %collective-permute-start.11 = (bf16[4,32,256]{2,1,0:T(8,128)(2,1)S(1)}, bf16[4,32,256]{2,1,0:T(8,128)(2,1)S(1)}, u32[]{:S(2)}, u32[]{:S(2)}) collective-permute-start(bf16[4,32,256]{2,1,0:T(8,128)(2,1)S(1)} %dynamic-slice_bitcast_fusion.1), channel_id=1, source_target_pairs={{0,128},{64,192},{128,0},{192,64},{1,129},{65,193},{129,1},{193,65... | collective-permute-start | bytes 196616 | tf_op jit(solution)/shard_map/ppermute | solution.py:221
  48.6 3.9 %collective-permute-start.10 = (bf16[4,32,256]{2,1,0:T(8,128)(2,1)S(1)}, bf16[4,32,256]{2,1,0:T(8,128)(2,1)S(1)}, u32[]{:S(2)}, u32[]{:S(2)}) collective-permute-start(bf16[4,32,256]{2,1,0:T(8,128)(2,1)S(1)} %dynamic-slice_bitcast_fusion.1), channel_id=1, source_target_pairs={{0,64},{64,0},{128,192},{192,128},{1,65},{65,1},{129,193},{193,129... | collective-permute-start | bytes 196616 | tf_op jit(solution)/shard_map/ppermute | solution.py:221
  52.7 4.4 %collective-permute-start.15 = (bf16[2,32,256]{2,1,0:T(8,128)(2,1)S(1)}, bf16[2,32,256]{2,1,0:T(8,128)(2,1)S(1)}, u32[]{:S(2)}, u32[]{:S(2)}) collective-permute-start(bf16[2,32,256]{2,1,0:T(8,128)(2,1)S(1)} %get-tuple-element.51), channel_id=1, source_target_pairs={{0,3},{1,2},{2,1},{3,0},{4,7},{5,6},{6,5},{7,4},{8,11},{9,10},{10,... | collective-permute-start | bytes 98312 | tf_op jit(solution)/shard_map/ppermute | solution.py:253
  54.4 4.6 %collective-permute-start.14 = (bf16[2,32,256]{2,1,0:T(8,128)(2,1)S(1)}, bf16[2,32,256]{2,1,0:T(8,128)(2,1)S(1)}, u32[]{:S(2)}, u32[]{:S(2)}) collective-permute-start(bf16[2,32,256]{2,1,0:T(8,128)(2,1)S(1)} %get-tuple-element.51), channel_id=1, source_target_pairs={{0,2},{1,3},{2,0},{3,1},{4,6},{5,7},{6,4},{7,5},{8,10},{9,11},{10,... | collective-permute-start | bytes 98312 | tf_op jit(solution)/shard_map/ppermute | solution.py:253
  69.9 4.3 %collective-permute-start.18 = (bf16[4,32,256]{2,1,0:T(8,128)(2,1)S(1)}, bf16[4,32,256]{2,1,0:T(8,128)(2,1)S(1)}, u32[]{:S(2)}, u32[]{:S(2)}) collective-permute-start(bf16[4,32,256]{2,1,0:T(8,128)(2,1)S(1)} %dynamic-slice_bitcast_fusion), channel_id=1, source_target_pairs={{0,192},{64,128},{128,64},{192,0},{1,193},{65,129},{129,65},{193,1... | collective-permute-start | bytes 196616 | tf_op jit(solution)/shard_map/ppermute | solution.py:221
  71.2 4.6 %collective-permute-start.17 = (bf16[4,32,256]{2,1,0:T(8,128)(2,1)S(1)}, bf16[4,32,256]{2,1,0:T(8,128)(2,1)S(1)}, u32[]{:S(2)}, u32[]{:S(2)}) collective-permute-start(bf16[4,32,256]{2,1,0:T(8,128)(2,1)S(1)} %dynamic-slice_bitcast_fusion), channel_id=1, source_target_pairs={{0,128},{64,192},{128,0},{192,64},{1,129},{65,193},{129,1},{193,65... | collective-permute-start | bytes 196616 | tf_op jit(solution)/shard_map/ppermute | solution.py:221
  71.7 4.2 %collective-permute-start.16 = (bf16[4,32,256]{2,1,0:T(8,128)(2,1)S(1)}, bf16[4,32,256]{2,1,0:T(8,128)(2,1)S(1)}, u32[]{:S(2)}, u32[]{:S(2)}) collective-permute-start(bf16[4,32,256]{2,1,0:T(8,128)(2,1)S(1)} %dynamic-slice_bitcast_fusion), channel_id=1, source_target_pairs={{0,64},{64,0},{128,192},{192,128},{1,65},{65,1},{129,193},{193,129... | collective-permute-start | bytes 196616 | tf_op jit(solution)/shard_map/ppermute | solution.py:221
  76.0 4.1 %collective-permute-start.21 = (bf16[2,32,256]{2,1,0:T(8,128)(2,1)S(1)}, bf16[2,32,256]{2,1,0:T(8,128)(2,1)S(1)}, u32[]{:S(2)}, u32[]{:S(2)}) collective-permute-start(bf16[2,32,256]{2,1,0:T(8,128)(2,1)S(1)} %get-tuple-element.53), channel_id=1, source_target_pairs={{0,3},{1,2},{2,1},{3,0},{4,7},{5,6},{6,5},{7,4},{8,11},{9,10},{10,... | collective-permute-start | bytes 98312 | tf_op jit(solution)/shard_map/ppermute | solution.py:253
  77.1 4.3 %collective-permute-start.20 = (bf16[2,32,256]{2,1,0:T(8,128)(2,1)S(1)}, bf16[2,32,256]{2,1,0:T(8,128)(2,1)S(1)}, u32[]{:S(2)}, u32[]{:S(2)}) collective-permute-start(bf16[2,32,256]{2,1,0:T(8,128)(2,1)S(1)} %get-tuple-element.53), channel_id=1, source_target_pairs={{0,2},{1,3},{2,0},{3,1},{4,6},{5,7},{6,4},{7,5},{8,10},{9,11},{10,... | collective-permute-start | bytes 98312 | tf_op jit(solution)/shard_map/ppermute | solution.py:253
  82.1 4.7 %collective-permute-start.24 = (bf16[4,32,256]{2,1,0:T(8,128)(2,1)S(1)}, bf16[4,32,256]{2,1,0:T(8,128)(2,1)S(1)}, u32[]{:S(2)}, u32[]{:S(2)}) collective-permute-start(bf16[4,32,256]{2,1,0:T(8,128)(2,1)S(1)} %get-tuple-element.60), channel_id=1, source_target_pairs={{0,192},{64,128},{128,64},{192,0},{1,193},{65,129},{129,65},{193,1... | collective-permute-start | bytes 196616 | tf_op jit(solution)/shard_map/ppermute | solution.py:277
  84.8 4.6 %collective-permute-start.23 = (bf16[4,32,256]{2,1,0:T(8,128)(2,1)S(1)}, bf16[4,32,256]{2,1,0:T(8,128)(2,1)S(1)}, u32[]{:S(2)}, u32[]{:S(2)}) collective-permute-start(bf16[4,32,256]{2,1,0:T(8,128)(2,1)S(1)} %get-tuple-element.59), channel_id=1, source_target_pairs={{0,128},{64,192},{128,0},{192,64},{1,129},{65,193},{129,1},{193,65... | collective-permute-start | bytes 196616 | tf_op jit(solution)/shard_map/ppermute | solution.py:277
  85.0 4.4 %collective-permute-start.22 = (bf16[4,32,256]{2,1,0:T(8,128)(2,1)S(1)}, bf16[4,32,256]{2,1,0:T(8,128)(2,1)S(1)}, u32[]{:S(2)}, u32[]{:S(2)}) collective-permute-start(bf16[4,32,256]{2,1,0:T(8,128)(2,1)S(1)} %get-tuple-element.58), channel_id=1, source_target_pairs={{0,64},{64,0},{128,192},{192,128},{1,65},{65,1},{129,193},{193,129... | collective-permute-start | bytes 196616 | tf_op jit(solution)/shard_map/ppermute | solution.py:277
  101.8 4.1 %collective-permute-start.26 = (bf16[32,256]{1,0:T(8,128)(2,1)S(1)}, bf16[32,256]{1,0:T(8,128)(2,1)S(1)}, u32[]{:S(2)}, u32[]{:S(2)}) collective-permute-start(bf16[32,256]{1,0:T(8,128)(2,1)S(1)} %convolution_convert_fusion.2), channel_id=1, source_target_pairs={{0,2},{1,3},{2,0},{3,1},{4,6},{5,7},{6,4},{7,5},{8,10},{9,11},{10,... | collective-permute-start | bytes 49160 | tf_op jit(solution)/shard_map/ppermute | solution.py:282
  106.0 4.4 %collective-permute-start.30 = (bf16[4,32,256]{2,1,0:T(8,128)(2,1)S(1)}, bf16[4,32,256]{2,1,0:T(8,128)(2,1)S(1)}, u32[]{:S(2)}, u32[]{:S(2)}) collective-permute-start(bf16[4,32,256]{2,1,0:T(8,128)(2,1)S(1)} %get-tuple-element.65), channel_id=1, source_target_pairs={{0,192},{64,128},{128,64},{192,0},{1,193},{65,129},{129,65},{193,1... | collective-permute-start | bytes 196616 | tf_op jit(solution)/shard_map/ppermute | solution.py:277
  107.1 4.6 %collective-permute-start.29 = (bf16[4,32,256]{2,1,0:T(8,128)(2,1)S(1)}, bf16[4,32,256]{2,1,0:T(8,128)(2,1)S(1)}, u32[]{:S(2)}, u32[]{:S(2)}) collective-permute-start(bf16[4,32,256]{2,1,0:T(8,128)(2,1)S(1)} %get-tuple-element.64), channel_id=1, source_target_pairs={{0,128},{64,192},{128,0},{192,64},{1,129},{65,193},{129,1},{193,65... | collective-permute-start | bytes 196616 | tf_op jit(solution)/shard_map/ppermute | solution.py:277
  108.0 4.0 %collective-permute-start.28 = (bf16[4,32,256]{2,1,0:T(8,128)(2,1)S(1)}, bf16[4,32,256]{2,1,0:T(8,128)(2,1)S(1)}, u32[]{:S(2)}, u32[]{:S(2)}) collective-permute-start(bf16[4,32,256]{2,1,0:T(8,128)(2,1)S(1)} %get-tuple-element.63), channel_id=1, source_target_pairs={{0,64},{64,0},{128,192},{192,128},{1,65},{65,1},{129,193},{193,129... | collective-permute-start | bytes 196616 | tf_op jit(solution)/shard_map/ppermute | solution.py:277
  122.5 3.8 %collective-permute-start.33 = (bf16[32,256]{1,0:T(8,128)(2,1)S(1)}, bf16[32,256]{1,0:T(8,128)(2,1)S(1)}, u32[]{:S(2)}, u32[]{:S(2)}) collective-permute-start(bf16[32,256]{1,0:T(8,128)(2,1)S(1)} %convolution_convert_fusion.1), channel_id=1, source_target_pairs={{0,3},{1,2},{2,1},{3,0},{4,7},{5,6},{6,5},{7,4},{8,11},{9,10},{10,... | collective-permute-start | bytes 49160 | tf_op jit(solution)/shard_map/ppermute | solution.py:282
  123.4 4.1 %collective-permute-start.32 = (bf16[32,256]{1,0:T(8,128)(2,1)S(1)}, bf16[32,256]{1,0:T(8,128)(2,1)S(1)}, u32[]{:S(2)}, u32[]{:S(2)}) collective-permute-start(bf16[32,256]{1,0:T(8,128)(2,1)S(1)} %convolution_convert_fusion.1), channel_id=1, source_target_pairs={{0,2},{1,3},{2,0},{3,1},{4,6},{5,7},{6,4},{7,5},{8,10},{9,11},{10,... | collective-permute-start | bytes 49160 | tf_op jit(solution)/shard_map/ppermute | solution.py:282
  127.8 4.4 %collective-permute-start.36 = (bf16[4,32,256]{2,1,0:T(8,128)(2,1)S(1)}, bf16[4,32,256]{2,1,0:T(8,128)(2,1)S(1)}, u32[]{:S(2)}, u32[]{:S(2)}) collective-permute-start(bf16[4,32,256]{2,1,0:T(8,128)(2,1)S(1)} %get-tuple-element.69), channel_id=1, source_target_pairs={{0,192},{64,128},{128,64},{192,0},{1,193},{65,129},{129,65},{193,1... | collective-permute-start | bytes 196616 | tf_op jit(solution)/shard_map/ppermute | solution.py:277
  129.5 4.6 %collective-permute-start.35 = (bf16[4,32,256]{2,1,0:T(8,128)(2,1)S(1)}, bf16[4,32,256]{2,1,0:T(8,128)(2,1)S(1)}, u32[]{:S(2)}, u32[]{:S(2)}) collective-permute-start(bf16[4,32,256]{2,1,0:T(8,128)(2,1)S(1)} %get-tuple-element.68), channel_id=1, source_target_pairs={{0,128},{64,192},{128,0},{192,64},{1,129},{65,193},{129,1},{193,65... | collective-permute-start | bytes 196616 | tf_op jit(solution)/shard_map/ppermute | solution.py:277
  144.6 4.1 %collective-permute-start.39 = (bf16[32,256]{1,0:T(8,128)(2,1)S(1)}, bf16[32,256]{1,0:T(8,128)(2,1)S(1)}, u32[]{:S(2)}, u32[]{:S(2)}) collective-permute-start(bf16[32,256]{1,0:T(8,128)(2,1)S(1)} %convolution_convert_fusion), channel_id=1, source_target_pairs={{0,3},{1,2},{2,1},{3,0},{4,7},{5,6},{6,5},{7,4},{8,11},{9,10},{10,... | collective-permute-start | bytes 49160 | tf_op jit(solution)/shard_map/ppermute | solution.py:282
  146.3 4.1 %collective-permute-start.38 = (bf16[32,256]{1,0:T(8,128)(2,1)S(1)}, bf16[32,256]{1,0:T(8,128)(2,1)S(1)}, u32[]{:S(2)}, u32[]{:S(2)}) collective-permute-start(bf16[32,256]{1,0:T(8,128)(2,1)S(1)} %convolution_convert_fusion), channel_id=1, source_target_pairs={{0,2},{1,3},{2,0},{3,1},{4,6},{5,7},{6,4},{7,5},{8,10},{9,11},{10,... | collective-permute-start | bytes 49160 | tf_op jit(solution)/shard_map/ppermute | solution.py:282
  150.5 26.6 %collective-permute-start.40 = (bf16[2,32,256]{2,1,0:T(8,128)(2,1)S(1)}, bf16[2,32,256]{2,1,0:T(8,128)(2,1)S(1)}, u32[]{:S(2)}, u32[]{:S(2)}) collective-permute-start(bf16[2,32,256]{2,1,0:T(8,128)(2,1)S(1)} %pad_maximum_fusion.8), channel_id=1, source_target_pairs={{0,4},{4,0},{1,5},{5,1},{2,6},{6,2},{3,7},{7,3},{8,12},{12,8},{9,1... | collective-permute-start | bytes 98312 | tf_op jit(solution)/shard_map/ppermute | solution.py:24
  (11 other events, 38.6 us)
where the time goes:
time: 178 us
  starting transfers between devices  75.9 us (43%)
  blocking collectives  51.7 us (29%)
  waiting for transfers between devices  40.6 us (23%)
  Pallas kernels  4.59 us (3%)
  matrix products  1.97 us (1%)
    all_to_all x3, blocking collectives, shards(): arrived = lax.all_to_all(out, 'z', 0, 0)  30.9 us
    ppermute x5, starting transfers between devices, swap(): return lax.ppermute(v, 'k', [(0, 1), (1, 0)])  29.7 us
    all_to_all x2, blocking collectives, shards(): lax.all_to_all(jnp.broadcast_to(sent[None], (NZ, half, width)), 'z', 0, 0)  20.8 us
    ppermute x9, starting transfers between devices, shards(): lax.ppermute(rows, 'y', pairs(NY, s)).astype(F32)  10.2 us
    ppermute x9, starting transfers between devices, shards(): mine = mine + lax.ppermute(parts[s - 1], 'x', pairs(NX, s)).astype(F32)  10 us
    ppermute x9, starting transfers between devices, shards(): lax.ppermute(o_r, 'y', pairs(NY, s))  9.8 us
    ppermute x9, starting transfers between devices, shards(): parts = [got] + [lax.ppermute(got, 'x', pairs(NX, s)) for s in (1, 2, 3)]  9.76 us
    ppermute x9, waiting for transfers between devices, shards(): mine = mine + lax.ppermute(parts[s - 1], 'x', pairs(NX, s)).astype(F32)  9.55 us
  transfers between devices with their start and end apart: 42, of which 26 were waited for; matrix products, arithmetic and copies ran while one was open for 1% of the time, Pallas kernels for 2%

commit v1 on v0

--- a/solution.py
+++ b/solution.py
@@ -140,21 +140,23 @@
     sent[1] = jnp.where(k == 0, p_out[1], p_out[0]).astype(BF16)
 
 
-def backward_products(level, plan, o_own, o_par, held, rest, t0, t1, t2, t3, total, spare, sem):
+def backward_products(level, plan, o_own, o_par, held, rest, sent, total, spare, sem):
+    x = lax.axis_index("x")
     total[...] = jnp.zeros_like(total)
     for r, solved in enumerate((o_own, o_par)):
 
         def use(n, block, solved=solved):
-            total[n] += jnp.dot(solved[...], block, preferred_element_type=F32)
+            total[block_column(x, n)] += jnp.dot(solved[...], block, preferred_element_type=F32)
 
         @pl.when(plan[ROWS + r] == level + 1)
         def _(r=r, use=use):
             at = BOUNDS + r * LEVELS
             use_blocks(plan, r, plan[at], plan[at + LEVELS], held, rest, spare, sem, use)
 
-    t0[...] = total[0:HZ]
-    for s, out in ((1, t1), (2, t2), (3, t3)):
-        out[...] = total[s * HZ : (s + 1) * HZ].astype(BF16)
+    for j in range(NX * HZ):
+        rows = total[j].astype(BF16)
+        sent[2 * j] = rows
+        sent[2 * j + 1] = rows
 
 
 def in_hbm(v):
@@ -265,18 +267,15 @@
     o_own, o_par, f_r, d_r = lax.optimization_barrier((o_own, o_par, f_r, d_r))
     r_sum = jnp.zeros((half, width), F32)
     for level in range(top - 1, -1, -1):
-        mine, *parts = pl.pallas_call(
+        sent = pl.pallas_call(
             functools.partial(backward_products, level),
             in_specs=[smem] + [vmem] * 3 + [anywhere],
-            out_specs=[vmem] * 4,
-            out_shape=[jax.ShapeDtypeStruct((HZ, half, width), t) for t in (F32, BF16, BF16, BF16)],
+            out_specs=vmem,
+            out_shape=jax.ShapeDtypeStruct((NX * NZ, half, width), BF16),
             scratch_shapes=[pltpu.VMEM((n_j, half, width), F32)] + fetch,
             compiler_params=params,
         )(plan, o_own, o_par, held, rest)
-        for s in (1, 2, 3):
-            mine = mine + lax.ppermute(parts[s - 1], "x", pairs(NX, s)).astype(F32)
-        out = jnp.broadcast_to(mine.astype(BF16)[:, None], (HZ, 2, half, width)).reshape(NZ, half, width)
-        arrived = lax.all_to_all(out, "z", 0, 0)
+        arrived = lax.all_to_all(sent, ("x", "z"), 0, 0)
         r_sum = r_sum + jnp.sum(arrived.astype(F32), axis=0)
         o_r = solve_t(f_r.astype(F32) - r_sum, d_r)
         got = jnp.stack([o_r] + [lax.ppermute(o_r, "y", pairs(NY, s)) for s in (1, 2, 3)])

time: 178 us -> 175 us (0.983)
  blocking collectives: 51.7 us -> 68.9 us
  starting transfers between devices: 75.9 us -> 59.8 us
  waiting for transfers between devices: 40.6 us -> 31.4 us
  Pallas kernels: 4.59 us -> 8.92 us
    all_to_all x3, blocking collectives: 30.9 us -> 48.3 us  [shards(): arrived = lax.all_to_all(sent, ('x', 'z'), 0, 0)]
    ppermute x9 -> x0, starting transfers between devices: 10 us -> none  [shards(): mine = mine + lax.ppermute(parts[s - 1], 'x', pairs(NX, s)).astype(F32)]
    ppermute x9 -> x0, waiting for transfers between devices: 9.55 us -> none  [shards(): mine = mine + lax.ppermute(parts[s - 1], 'x', pairs(NX, s)).astype(F32)]
    ppermute x5, starting transfers between devices: 29.7 us -> 23.8 us  [swap(): return lax.ppermute(v, 'k', [(0, 1), (1, 0)])]
    pallas_call x3, Pallas kernels: 0.32 us -> 2.39 us  [shards(): pl.pallas_call(functools.partial(forward_products, level), in_specs=[smem...]
  transfers between devices with their start and end apart: 42 -> 33, of which waited for: 26 -> 22; matrix products, arithmetic and copies ran while one was open for 1% -> 1% of each run, Pallas kernels for 2% -> 3%
where the time goes in v1:
time: 175 us; the launch traced here: 174 us
  blocking collectives  68.9 us (39%)
  starting transfers between devices  59.8 us (34%)
  waiting for transfers between devices  31.4 us (18%)
  Pallas kernels  8.92 us (5%)
  matrix products  1.97 us (1%)
    all_to_all x3, blocking collectives, shards(): arrived = lax.all_to_all(sent, ('x', 'z'), 0, 0)  48.3 us
    ppermute x5, starting transfers between devices, swap(): return lax.ppermute(v, 'k', [(0, 1), (1, 0)])  23.8 us
    all_to_all x2, blocking collectives, shards(): lax.all_to_all(jnp.broadcast_to(sent[None], (NZ, half, width)), 'z', 0, 0)  20.6 us
    ppermute x9, starting transfers between devices, shards(): lax.ppermute(rows, 'y', pairs(NY, s)).astype(F32)  10 us
    ppermute x9, starting transfers between devices, shards(): lax.ppermute(o_r, 'y', pairs(NY, s))  9.8 us
    ppermute x9, starting transfers between devices, shards(): parts = [got] + [lax.ppermute(got, 'x', pairs(NX, s)) for s in (1, 2, 3)]  9.76 us
    ppermute x9, waiting for transfers between devices, shards(): lax.ppermute(rows, 'y', pairs(NY, s)).astype(F32)  8.75 us
    all_to_all x1, waiting for transfers between devices, shards(): lax.all_to_all(jnp.broadcast_to(sent[None], (NZ, half, width)), 'z', 0, 0)  7.84 us
  transfers between devices with their start and end apart: 33, of which 22 were waited for; matrix products, arithmetic and copies ran while one was open for 1% of the time, Pallas kernels for 3%

profile of v1, /device:TPU:1, one launch (start us, length us, event | category | flops | bytes accessed | tf_op | source)
XLA Modules:
  0.0 173.9 jit_solution(16666609929139640753)
XLA Ops:
  0.6 3.3 %collective-permute-start = (bf16[256,256]{1,0:T(8,128)(2,1)}, bf16[256,256]{1,0:T(8,128)(2,1)S(1)}, u32[]{:S(2)}, u32[]{:S(2)}) collective-permute-start(bf16[256,256]{1,0:T(8,128)(2,1)} %bitcast.125), channel_id=1, source_target_pairs={{0,4},{4,0},{1,5},{5,1},{2,6},{6,2},{3,7},{7,3},{8,12},{12,8},{9,1... | collective-permute-start | bytes 393224 | tf_op jit(solution)/shard_map/ppermute | solution.py:24
  4.5 1.1 shard_map.68
  6.7 6.5 %all-to-all-start = ((bf16[8,32,256]{2,1,0:T(8,128)(2,1)}), bf16[8,32,256]{2,1,0:T(8,128)(2,1)S(1)}, u32[]{:S(2)}, u32[]{:S(2)}) async-start(bf16[8,32,256]{2,1,0:T(8,128)(2,1)} %broadcast_in_dim.11), calls=%async_computation | async-start | bytes 262144 | tf_op jit(solution)/shard_map/all_to_all | solution.py:221
  13.2 7.8 %all-to-all-done = bf16[8,32,256]{2,1,0:T(8,128)(2,1)S(1)} async-done(((bf16[8,32,256]{2,1,0:T(8,128)(2,1)}), bf16[8,32,256]{2,1,0:T(8,128)(2,1)S(1)}, u32[]{:S(2)}, u32[]{:S(2)}) %all-to-all-start) | async-done | bytes 131104 | tf_op jit(solution)/shard_map/all_to_all | solution.py:221
  21.0 2.5 %collective-permute-start.6 = (bf16[4,32,256]{2,1,0:T(8,128)(2,1)S(1)}, bf16[4,32,256]{2,1,0:T(8,128)(2,1)S(1)}, u32[]{:S(2)}, u32[]{:S(2)}) collective-permute-start(bf16[4,32,256]{2,1,0:T(8,128)(2,1)S(1)} %dynamic-slice_bitcast_fusion.2.here), channel_id=1, source_target_pairs={{0,192},{64,128},{128,64},{192,0},{1,193},{65,129},{129,65},{193,1... | collective-permute-start | bytes 196616 | tf_op jit(solution)/shard_map/ppermute | solution.py:223
  24.3 3.3 %shard_map.69 = (s32[44]{0:T(128)S(4)}, bf16[20,256,256]{2,1,0:T(8,128)(2,1)S(1)}, bf16[12,256,256]{2,1,0:T(8,128)(2,1)}, bf16[4,32,256]{2,1,0:T(8,128)(2,1)S(1)}) custom-call(s32[64]{0:T(128)} %levels_hbm.3, s32[16]{0:T(128)} %bitcast.149, s32[16]{0:T(128)S(1)} %collective-permute-done.2.pattern_par, bf16[16,256,256]{2,1,0:T(8,128)(2,1)} %bitcast.128, ...), custom_call_target="tpu_custom_call" | custom-call | tf_op jit(solution)/shard_map/pallas_call | solution.py:225
  28.3 1.2 shard_map.70
  29.5 2.6 %collective-permute-start.9 = (bf16[2,32,256]{2,1,0:T(8,128)(2,1)S(1)}, bf16[2,32,256]{2,1,0:T(8,128)(2,1)S(1)}, u32[]{:S(2)}, u32[]{:S(2)}) collective-permute-start(bf16[2,32,256]{2,1,0:T(8,128)(2,1)S(1)} %get-tuple-element.37), channel_id=1, source_target_pairs={{0,3},{1,2},{2,1},{3,0},{4,7},{5,6},{6,5},{7,4},{8,11},{9,10},{10,... | collective-permute-start | bytes 98312 | tf_op jit(solution)/shard_map/ppermute | solution.py:255
  33.5 2.8 %collective-permute-done.8 = bf16[2,32,256]{2,1,0:T(8,128)(2,1)S(1)} collective-permute-done((bf16[2,32,256]{2,1,0:T(8,128)(2,1)S(1)}, bf16[2,32,256]{2,1,0:T(8,128)(2,1)S(1)}, u32[]{:S(2)}, u32[]{:S(2)}) %collective-permute-start.8) | collective-permute-done | bytes 32800 | tf_op jit(solution)/shard_map/ppermute | solution.py:255
  36.8 10.3 %all_to_all.30 = bf16[8,32,256]{2,1,0:T(8,128)(2,1)S(1)} all-to-all(bf16[8,32,256]{2,1,0:T(8,128)(2,1)S(1)} %broadcast_in_dim.13), channel_id=1, replica_groups=mesh['x'=4,'z'=8,'k'=2,'y'=4] {'z'}, dimensions={0} | all-to-all | bytes 262144 | tf_op jit(solution)/shard_map/all_to_all | solution.py:221
  47.1 1.6 collective-permute-start.12
  48.7 1.1 collective-permute-start.11
  50.4 1.4 collective-permute-done.12
  51.7 1.6 collective-permute-done.11
  54.5 2.3 %collective-permute-start.14 = (bf16[2,32,256]{2,1,0:T(8,128)(2,1)S(1)}, bf16[2,32,256]{2,1,0:T(8,128)(2,1)S(1)}, u32[]{:S(2)}, u32[]{:S(2)}) collective-permute-start(bf16[2,32,256]{2,1,0:T(8,128)(2,1)S(1)} %get-tuple-element.39), channel_id=1, source_target_pairs={{0,2},{1,3},{2,0},{3,1},{4,6},{5,7},{6,4},{7,5},{8,10},{9,11},{10,... | collective-permute-start | bytes 98312 | tf_op jit(solution)/shard_map/ppermute | solution.py:255
  60.3 10.3 %all_to_all.31 = bf16[8,32,256]{2,1,0:T(8,128)(2,1)S(1)} all-to-all(bf16[8,32,256]{2,1,0:T(8,128)(2,1)S(1)} %broadcast_in_dim.28), channel_id=1, replica_groups=mesh['x'=4,'z'=8,'k'=2,'y'=4] {'z'}, dimensions={0} | all-to-all | bytes 262144 | tf_op jit(solution)/shard_map/all_to_all | solution.py:221
  72.5 1.4 collective-permute-start.16
  73.9 1.1 collective-permute-done.18
  74.9 1.1 collective-permute-done.17
  76.8 2.1 %collective-permute-start.21 = (bf16[2,32,256]{2,1,0:T(8,128)(2,1)S(1)}, bf16[2,32,256]{2,1,0:T(8,128)(2,1)S(1)}, u32[]{:S(2)}, u32[]{:S(2)}) collective-permute-start(bf16[2,32,256]{2,1,0:T(8,128)(2,1)S(1)} %get-tuple-element.41), channel_id=1, source_target_pairs={{0,3},{1,2},{2,1},{3,0},{4,7},{5,6},{6,5},{7,4},{8,11},{9,10},{10,... | collective-permute-start | bytes 98312 | tf_op jit(solution)/shard_map/ppermute | solution.py:255
  80.8 2.4 %collective-permute-done.20 = bf16[2,32,256]{2,1,0:T(8,128)(2,1)S(1)} collective-permute-done((bf16[2,32,256]{2,1,0:T(8,128)(2,1)S(1)}, bf16[2,32,256]{2,1,0:T(8,128)(2,1)S(1)}, u32[]{:S(2)}, u32[]{:S(2)}) %collective-permute-start.20) | collective-permute-done | bytes 32800 | tf_op jit(solution)/shard_map/ppermute | solution.py:255
  84.8 15.1 %all_to_all.32 = bf16[32,32,256]{2,1,0:T(8,128)(2,1)S(1)} all-to-all(bf16[32,32,256]{2,1,0:T(8,128)(2,1)S(1)} %shard_map.73), channel_id=1, replica_groups=mesh['x'=4,'z'=8,'k'=2,'y'=4] {'x','z'}, dimensions={0} | all-to-all | bytes 1048576 | tf_op jit(solution)/shard_map/all_to_all | solution.py:278
  100.5 1.3 collective-permute-start.23
  101.8 1.6 collective-permute-start.22
  104.9 1.1 shard_map.74
  106.1 16.0 %all_to_all.33 = bf16[32,32,256]{2,1,0:T(8,128)(2,1)S(1)} all-to-all(bf16[32,32,256]{2,1,0:T(8,128)(2,1)S(1)} %shard_map.74), channel_id=1, replica_groups=mesh['x'=4,'z'=8,'k'=2,'y'=4] {'x','z'}, dimensions={0} | all-to-all | bytes 1048576 | tf_op jit(solution)/shard_map/all_to_all | solution.py:278
  122.4 2.2 %collective-permute-start.27 = (bf16[32,256]{1,0:T(8,128)(2,1)S(1)}, bf16[32,256]{1,0:T(8,128)(2,1)S(1)}, u32[]{:S(2)}, u32[]{:S(2)}) collective-permute-start(bf16[32,256]{1,0:T(8,128)(2,1)S(1)} %convolution_convert_fusion.1), channel_id=1, source_target_pairs={{0,3},{1,2},{2,1},{3,0},{4,7},{5,6},{6,5},{7,4},{8,11},{9,10},{10,... | collective-permute-start | bytes 49160 | tf_op jit(solution)/shard_map/ppermute | solution.py:281
  126.2 2.5 %collective-permute-done.26 = bf16[32,256]{1,0:T(8,128)(2,1)S(1)} collective-permute-done((bf16[32,256]{1,0:T(8,128)(2,1)S(1)}, bf16[32,256]{1,0:T(8,128)(2,1)S(1)}, u32[]{:S(2)}, u32[]{:S(2)}) %collective-permute-start.26) | collective-permute-done | bytes 16416 | tf_op jit(solution)/shard_map/ppermute | solution.py:281
  128.8 17.2 %all_to_all.34 = bf16[32,32,256]{2,1,0:T(8,128)(2,1)S(1)} all-to-all(bf16[32,32,256]{2,1,0:T(8,128)(2,1)S(1)} %shard_map.75), channel_id=1, replica_groups=mesh['x'=4,'z'=8,'k'=2,'y'=4] {'x','z'}, dimensions={0} | all-to-all | bytes 1048576 | tf_op jit(solution)/shard_map/all_to_all | solution.py:278
  146.2 2.2 %collective-permute-start.30 = (bf16[32,256]{1,0:T(8,128)(2,1)S(1)}, bf16[32,256]{1,0:T(8,128)(2,1)S(1)}, u32[]{:S(2)}, u32[]{:S(2)}) collective-permute-start(bf16[32,256]{1,0:T(8,128)(2,1)S(1)} %convolution_convert_fusion), channel_id=1, source_target_pairs={{0,3},{1,2},{2,1},{3,0},{4,7},{5,6},{6,5},{7,4},{8,11},{9,10},{10,... | collective-permute-start | bytes 49160 | tf_op jit(solution)/shard_map/ppermute | solution.py:281
  150.0 2.5 %collective-permute-done.29 = bf16[32,256]{1,0:T(8,128)(2,1)S(1)} collective-permute-done((bf16[32,256]{1,0:T(8,128)(2,1)S(1)}, bf16[32,256]{1,0:T(8,128)(2,1)S(1)}, u32[]{:S(2)}, u32[]{:S(2)}) %collective-permute-start.29) | collective-permute-done | bytes 16416 | tf_op jit(solution)/shard_map/ppermute | solution.py:281
  152.6 19.8 %collective-permute-start.31 = (bf16[2,32,256]{2,1,0:T(8,128)(2,1)S(1)}, bf16[2,32,256]{2,1,0:T(8,128)(2,1)S(1)}, u32[]{:S(2)}, u32[]{:S(2)}) collective-permute-start(bf16[2,32,256]{2,1,0:T(8,128)(2,1)S(1)} %pad_maximum_fusion.8), channel_id=1, source_target_pairs={{0,4},{4,0},{1,5},{5,1},{2,6},{6,2},{3,7},{7,3},{8,12},{12,8},{9,1... | collective-permute-start | bytes 98312 | tf_op jit(solution)/shard_map/ppermute | solution.py:24
  (89 shorter events, 23.6 us)
Async XLA Ops:
  0.6 5.0 %collective-permute-start = (bf16[256,256]{1,0:T(8,128)(2,1)}, bf16[256,256]{1,0:T(8,128)(2,1)S(1)}, u32[]{:S(2)}, u32[]{:S(2)}) collective-permute-start(bf16[256,256]{1,0:T(8,128)(2,1)} %bitcast.125), channel_id=1, source_target_pairs={{0,4},{4,0},{1,5},{5,1},{2,6},{6,2},{3,7},{7,3},{8,12},{12,8},{9,1... | collective-permute-start | bytes 393224 | tf_op jit(solution)/shard_map/ppermute | solution.py:24
  4.0 1.7 collective-permute-start.1
  5.6 18.6 %collective-permute-start.3 = (bf16[16,256,256]{2,1,0:T(8,128)(2,1)}, bf16[16,256,256]{2,1,0:T(8,128)(2,1)}, u32[]{:S(2)}, u32[]{:S(2)}) collective-permute-start(bf16[16,256,256]{2,1,0:T(8,128)(2,1)} %bitcast.127), channel_id=1, source_target_pairs={{0,4},{4,0},{1,5},{5,1},{2,6},{6,2},{3,7},{7,3},{8,12},{12,8},{9,1... | collective-permute-start | bytes 6291464 | tf_op jit(solution)/shard_map/ppermute | solution.py:24
  6.7 14.3 %all-to-all-start = ((bf16[8,32,256]{2,1,0:T(8,128)(2,1)}), bf16[8,32,256]{2,1,0:T(8,128)(2,1)S(1)}, u32[]{:S(2)}, u32[]{:S(2)}) async-start(bf16[8,32,256]{2,1,0:T(8,128)(2,1)} %broadcast_in_dim.11), calls=%async_computation | async-start | bytes 262144 | tf_op jit(solution)/shard_map/all_to_all | solution.py:221
  21.0 6.6 %collective-permute-start.6 = (bf16[4,32,256]{2,1,0:T(8,128)(2,1)S(1)}, bf16[4,32,256]{2,1,0:T(8,128)(2,1)S(1)}, u32[]{:S(2)}, u32[]{:S(2)}) collective-permute-start(bf16[4,32,256]{2,1,0:T(8,128)(2,1)S(1)} %dynamic-slice_bitcast_fusion.2.here), channel_id=1, source_target_pairs={{0,192},{64,128},{128,64},{192,0},{1,193},{65,129},{129,65},{193,1... | collective-permute-start | bytes 196616 | tf_op jit(solution)/shard_map/ppermute | solution.py:223
  23.5 4.7 %collective-permute-start.5 = (bf16[4,32,256]{2,1,0:T(8,128)(2,1)S(1)}, bf16[4,32,256]{2,1,0:T(8,128)(2,1)S(1)}, u32[]{:S(2)}, u32[]{:S(2)}) collective-permute-start(bf16[4,32,256]{2,1,0:T(8,128)(2,1)S(1)} %dynamic-slice_bitcast_fusion.2.here), channel_id=1, source_target_pairs={{0,128},{64,192},{128,0},{192,64},{1,129},{65,193},{129,1},{193,65... | collective-permute-start | bytes 196616 | tf_op jit(solution)/shard_map/ppermute | solution.py:223
  24.0 4.2 %collective-permute-start.4 = (bf16[4,32,256]{2,1,0:T(8,128)(2,1)S(1)}, bf16[4,32,256]{2,1,0:T(8,128)(2,1)S(1)}, u32[]{:S(2)}, u32[]{:S(2)}) collective-permute-start(bf16[4,32,256]{2,1,0:T(8,128)(2,1)S(1)} %dynamic-slice_bitcast_fusion.2.here), channel_id=1, source_target_pairs={{0,64},{64,0},{128,192},{192,128},{1,65},{65,1},{129,193},{193,129... | collective-permute-start | bytes 196616 | tf_op jit(solution)/shard_map/ppermute | solution.py:223
  29.5 4.1 %collective-permute-start.9 = (bf16[2,32,256]{2,1,0:T(8,128)(2,1)S(1)}, bf16[2,32,256]{2,1,0:T(8,128)(2,1)S(1)}, u32[]{:S(2)}, u32[]{:S(2)}) collective-permute-start(bf16[2,32,256]{2,1,0:T(8,128)(2,1)S(1)} %get-tuple-element.37), channel_id=1, source_target_pairs={{0,3},{1,2},{2,1},{3,0},{4,7},{5,6},{6,5},{7,4},{8,11},{9,10},{10,... | collective-permute-start | bytes 98312 | tf_op jit(solution)/shard_map/ppermute | solution.py:255
  32.1 4.3 %collective-permute-start.8 = (bf16[2,32,256]{2,1,0:T(8,128)(2,1)S(1)}, bf16[2,32,256]{2,1,0:T(8,128)(2,1)S(1)}, u32[]{:S(2)}, u32[]{:S(2)}) collective-permute-start(bf16[2,32,256]{2,1,0:T(8,128)(2,1)S(1)} %get-tuple-element.37), channel_id=1, source_target_pairs={{0,2},{1,3},{2,0},{3,1},{4,6},{5,7},{6,4},{7,5},{8,10},{9,11},{10,... | collective-permute-start | bytes 98312 | tf_op jit(solution)/shard_map/ppermute | solution.py:255
  32.1 4.3 %collective-permute-start.7 = (bf16[2,32,256]{2,1,0:T(8,128)(2,1)S(1)}, bf16[2,32,256]{2,1,0:T(8,128)(2,1)S(1)}, u32[]{:S(2)}, u32[]{:S(2)}) collective-permute-start(bf16[2,32,256]{2,1,0:T(8,128)(2,1)S(1)} %get-tuple-element.37), channel_id=1, source_target_pairs={{0,1},{1,0},{2,3},{3,2},{4,5},{5,4},{6,7},{7,6},{8,9},{9,8},{10,11... | collective-permute-start | bytes 98312 | tf_op jit(solution)/shard_map/ppermute | solution.py:255
  47.1 4.6 %collective-permute-start.12 = (bf16[4,32,256]{2,1,0:T(8,128)(2,1)S(1)}, bf16[4,32,256]{2,1,0:T(8,128)(2,1)S(1)}, u32[]{:S(2)}, u32[]{:S(2)}) collective-permute-start(bf16[4,32,256]{2,1,0:T(8,128)(2,1)S(1)} %dynamic-slice_bitcast_fusion.1), channel_id=1, source_target_pairs={{0,192},{64,128},{128,64},{192,0},{1,193},{65,129},{129,65},{193,1... | collective-permute-start | bytes 196616 | tf_op jit(solution)/shard_map/ppermute | solution.py:223
  48.7 4.6 %collective-permute-start.11 = (bf16[4,32,256]{2,1,0:T(8,128)(2,1)S(1)}, bf16[4,32,256]{2,1,0:T(8,128)(2,1)S(1)}, u32[]{:S(2)}, u32[]{:S(2)}) collective-permute-start(bf16[4,32,256]{2,1,0:T(8,128)(2,1)S(1)} %dynamic-slice_bitcast_fusion.1), channel_id=1, source_target_pairs={{0,128},{64,192},{128,0},{192,64},{1,129},{65,193},{129,1},{193,65... | collective-permute-start | bytes 196616 | tf_op jit(solution)/shard_map/ppermute | solution.py:223
  49.9 3.5 %collective-permute-start.10 = (bf16[4,32,256]{2,1,0:T(8,128)(2,1)S(1)}, bf16[4,32,256]{2,1,0:T(8,128)(2,1)S(1)}, u32[]{:S(2)}, u32[]{:S(2)}) collective-permute-start(bf16[4,32,256]{2,1,0:T(8,128)(2,1)S(1)} %dynamic-slice_bitcast_fusion.1), channel_id=1, source_target_pairs={{0,64},{64,0},{128,192},{192,128},{1,65},{65,1},{129,193},{193,129... | collective-permute-start | bytes 196616 | tf_op jit(solution)/shard_map/ppermute | solution.py:223
  54.4 4.1 %collective-permute-start.15 = (bf16[2,32,256]{2,1,0:T(8,128)(2,1)S(1)}, bf16[2,32,256]{2,1,0:T(8,128)(2,1)S(1)}, u32[]{:S(2)}, u32[]{:S(2)}) collective-permute-start(bf16[2,32,256]{2,1,0:T(8,128)(2,1)S(1)} %get-tuple-element.39), channel_id=1, source_target_pairs={{0,3},{1,2},{2,1},{3,0},{4,7},{5,6},{6,5},{7,4},{8,11},{9,10},{10,... | collective-permute-start | bytes 98312 | tf_op jit(solution)/shard_map/ppermute | solution.py:255
  54.5 4.3 %collective-permute-start.14 = (bf16[2,32,256]{2,1,0:T(8,128)(2,1)S(1)}, bf16[2,32,256]{2,1,0:T(8,128)(2,1)S(1)}, u32[]{:S(2)}, u32[]{:S(2)}) collective-permute-start(bf16[2,32,256]{2,1,0:T(8,128)(2,1)S(1)} %get-tuple-element.39), channel_id=1, source_target_pairs={{0,2},{1,3},{2,0},{3,1},{4,6},{5,7},{6,4},{7,5},{8,10},{9,11},{10,... | collective-permute-start | bytes 98312 | tf_op jit(solution)/shard_map/ppermute | solution.py:255
  56.8 3.1 %collective-permute-start.13 = (bf16[2,32,256]{2,1,0:T(8,128)(2,1)S(1)}, bf16[2,32,256]{2,1,0:T(8,128)(2,1)S(1)}, u32[]{:S(2)}, u32[]{:S(2)}) collective-permute-start(bf16[2,32,256]{2,1,0:T(8,128)(2,1)S(1)} %get-tuple-element.39), channel_id=1, source_target_pairs={{0,1},{1,0},{2,3},{3,2},{4,5},{5,4},{6,7},{7,6},{8,9},{9,8},{10,11... | collective-permute-start | bytes 98312 | tf_op jit(solution)/shard_map/ppermute | solution.py:255
  70.6 4.3 %collective-permute-start.18 = (bf16[4,32,256]{2,1,0:T(8,128)(2,1)S(1)}, bf16[4,32,256]{2,1,0:T(8,128)(2,1)S(1)}, u32[]{:S(2)}, u32[]{:S(2)}) collective-permute-start(bf16[4,32,256]{2,1,0:T(8,128)(2,1)S(1)} %dynamic-slice_bitcast_fusion), channel_id=1, source_target_pairs={{0,192},{64,128},{128,64},{192,0},{1,193},{65,129},{129,65},{193,1... | collective-permute-start | bytes 196616 | tf_op jit(solution)/shard_map/ppermute | solution.py:223
  71.5 4.6 %collective-permute-start.17 = (bf16[4,32,256]{2,1,0:T(8,128)(2,1)S(1)}, bf16[4,32,256]{2,1,0:T(8,128)(2,1)S(1)}, u32[]{:S(2)}, u32[]{:S(2)}) collective-permute-start(bf16[4,32,256]{2,1,0:T(8,128)(2,1)S(1)} %dynamic-slice_bitcast_fusion), channel_id=1, source_target_pairs={{0,128},{64,192},{128,0},{192,64},{1,129},{65,193},{129,1},{193,65... | collective-permute-start | bytes 196616 | tf_op jit(solution)/shard_map/ppermute | solution.py:223
  72.5 4.0 %collective-permute-start.16 = (bf16[4,32,256]{2,1,0:T(8,128)(2,1)S(1)}, bf16[4,32,256]{2,1,0:T(8,128)(2,1)S(1)}, u32[]{:S(2)}, u32[]{:S(2)}) collective-permute-start(bf16[4,32,256]{2,1,0:T(8,128)(2,1)S(1)} %dynamic-slice_bitcast_fusion), channel_id=1, source_target_pairs={{0,64},{64,0},{128,192},{192,128},{1,65},{65,1},{129,193},{193,129... | collective-permute-start | bytes 196616 | tf_op jit(solution)/shard_map/ppermute | solution.py:223
  76.8 4.1 %collective-permute-start.21 = (bf16[2,32,256]{2,1,0:T(8,128)(2,1)S(1)}, bf16[2,32,256]{2,1,0:T(8,128)(2,1)S(1)}, u32[]{:S(2)}, u32[]{:S(2)}) collective-permute-start(bf16[2,32,256]{2,1,0:T(8,128)(2,1)S(1)} %get-tuple-element.41), channel_id=1, source_target_pairs={{0,3},{1,2},{2,1},{3,0},{4,7},{5,6},{6,5},{7,4},{8,11},{9,10},{10,... | collective-permute-start | bytes 98312 | tf_op jit(solution)/shard_map/ppermute | solution.py:255
  78.9 4.3 %collective-permute-start.20 = (bf16[2,32,256]{2,1,0:T(8,128)(2,1)S(1)}, bf16[2,32,256]{2,1,0:T(8,128)(2,1)S(1)}, u32[]{:S(2)}, u32[]{:S(2)}) collective-permute-start(bf16[2,32,256]{2,1,0:T(8,128)(2,1)S(1)} %get-tuple-element.41), channel_id=1, source_target_pairs={{0,2},{1,3},{2,0},{3,1},{4,6},{5,7},{6,4},{7,5},{8,10},{9,11},{10,... | collective-permute-start | bytes 98312 | tf_op jit(solution)/shard_map/ppermute | solution.py:255
  79.5 3.8 %collective-permute-start.19 = (bf16[2,32,256]{2,1,0:T(8,128)(2,1)S(1)}, bf16[2,32,256]{2,1,0:T(8,128)(2,1)S(1)}, u32[]{:S(2)}, u32[]{:S(2)}) collective-permute-start(bf16[2,32,256]{2,1,0:T(8,128)(2,1)S(1)} %get-tuple-element.41), channel_id=1, source_target_pairs={{0,1},{1,0},{2,3},{3,2},{4,5},{5,4},{6,7},{7,6},{8,9},{9,8},{10,11... | collective-permute-start | bytes 98312 | tf_op jit(solution)/shard_map/ppermute | solution.py:255
  100.1 3.8 %collective-permute-start.24 = (bf16[32,256]{1,0:T(8,128)(2,1)S(1)}, bf16[32,256]{1,0:T(8,128)(2,1)S(1)}, u32[]{:S(2)}, u32[]{:S(2)}) collective-permute-start(bf16[32,256]{1,0:T(8,128)(2,1)S(1)} %convolution_convert_fusion.2), channel_id=1, source_target_pairs={{0,3},{1,2},{2,1},{3,0},{4,7},{5,6},{6,5},{7,4},{8,11},{9,10},{10,... | collective-permute-start | bytes 49160 | tf_op jit(solution)/shard_map/ppermute | solution.py:281
  100.5 4.1 %collective-permute-start.23 = (bf16[32,256]{1,0:T(8,128)(2,1)S(1)}, bf16[32,256]{1,0:T(8,128)(2,1)S(1)}, u32[]{:S(2)}, u32[]{:S(2)}) collective-permute-start(bf16[32,256]{1,0:T(8,128)(2,1)S(1)} %convolution_convert_fusion.2), channel_id=1, source_target_pairs={{0,2},{1,3},{2,0},{3,1},{4,6},{5,7},{6,4},{7,5},{8,10},{9,11},{10,... | collective-permute-start | bytes 49160 | tf_op jit(solution)/shard_map/ppermute | solution.py:281
  101.8 3.1 %collective-permute-start.22 = (bf16[32,256]{1,0:T(8,128)(2,1)S(1)}, bf16[32,256]{1,0:T(8,128)(2,1)S(1)}, u32[]{:S(2)}, u32[]{:S(2)}) collective-permute-start(bf16[32,256]{1,0:T(8,128)(2,1)S(1)} %convolution_convert_fusion.2), channel_id=1, source_target_pairs={{0,1},{1,0},{2,3},{3,2},{4,5},{5,4},{6,7},{7,6},{8,9},{9,8},{10,11... | collective-permute-start | bytes 49160 | tf_op jit(solution)/shard_map/ppermute | solution.py:281
  122.4 3.8 %collective-permute-start.27 = (bf16[32,256]{1,0:T(8,128)(2,1)S(1)}, bf16[32,256]{1,0:T(8,128)(2,1)S(1)}, u32[]{:S(2)}, u32[]{:S(2)}) collective-permute-start(bf16[32,256]{1,0:T(8,128)(2,1)S(1)} %convolution_convert_fusion.1), channel_id=1, source_target_pairs={{0,3},{1,2},{2,1},{3,0},{4,7},{5,6},{6,5},{7,4},{8,11},{9,10},{10,... | collective-permute-start | bytes 49160 | tf_op jit(solution)/shard_map/ppermute | solution.py:281
  124.6 4.1 %collective-permute-start.26 = (bf16[32,256]{1,0:T(8,128)(2,1)S(1)}, bf16[32,256]{1,0:T(8,128)(2,1)S(1)}, u32[]{:S(2)}, u32[]{:S(2)}) collective-permute-start(bf16[32,256]{1,0:T(8,128)(2,1)S(1)} %convolution_convert_fusion.1), channel_id=1, source_target_pairs={{0,2},{1,3},{2,0},{3,1},{4,6},{5,7},{6,4},{7,5},{8,10},{9,11},{10,... | collective-permute-start | bytes 49160 | tf_op jit(solution)/shard_map/ppermute | solution.py:281
  125.2 3.5 %collective-permute-start.25 = (bf16[32,256]{1,0:T(8,128)(2,1)S(1)}, bf16[32,256]{1,0:T(8,128)(2,1)S(1)}, u32[]{:S(2)}, u32[]{:S(2)}) collective-permute-start(bf16[32,256]{1,0:T(8,128)(2,1)S(1)} %convolution_convert_fusion.1), channel_id=1, source_target_pairs={{0,1},{1,0},{2,3},{3,2},{4,5},{5,4},{6,7},{7,6},{8,9},{9,8},{10,11... | collective-permute-start | bytes 49160 | tf_op jit(solution)/shard_map/ppermute | solution.py:281
  146.2 3.8 %collective-permute-start.30 = (bf16[32,256]{1,0:T(8,128)(2,1)S(1)}, bf16[32,256]{1,0:T(8,128)(2,1)S(1)}, u32[]{:S(2)}, u32[]{:S(2)}) collective-permute-start(bf16[32,256]{1,0:T(8,128)(2,1)S(1)} %convolution_convert_fusion), channel_id=1, source_target_pairs={{0,3},{1,2},{2,1},{3,0},{4,7},{5,6},{6,5},{7,4},{8,11},{9,10},{10,... | collective-permute-start | bytes 49160 | tf_op jit(solution)/shard_map/ppermute | solution.py:281
  148.5 4.1 %collective-permute-start.29 = (bf16[32,256]{1,0:T(8,128)(2,1)S(1)}, bf16[32,256]{1,0:T(8,128)(2,1)S(1)}, u32[]{:S(2)}, u32[]{:S(2)}) collective-permute-start(bf16[32,256]{1,0:T(8,128)(2,1)S(1)} %convolution_convert_fusion), channel_id=1, source_target_pairs={{0,2},{1,3},{2,0},{3,1},{4,6},{5,7},{6,4},{7,5},{8,10},{9,11},{10,... | collective-permute-start | bytes 49160 | tf_op jit(solution)/shard_map/ppermute | solution.py:281
  149.2 3.3 %collective-permute-start.28 = (bf16[32,256]{1,0:T(8,128)(2,1)S(1)}, bf16[32,256]{1,0:T(8,128)(2,1)S(1)}, u32[]{:S(2)}, u32[]{:S(2)}) collective-permute-start(bf16[32,256]{1,0:T(8,128)(2,1)S(1)} %convolution_convert_fusion), channel_id=1, source_target_pairs={{0,1},{1,0},{2,3},{3,2},{4,5},{5,4},{6,7},{7,6},{8,9},{9,8},{10,11... | collective-permute-start | bytes 49160 | tf_op jit(solution)/shard_map/ppermute | solution.py:281
  152.6 20.6 %collective-permute-start.31 = (bf16[2,32,256]{2,1,0:T(8,128)(2,1)S(1)}, bf16[2,32,256]{2,1,0:T(8,128)(2,1)S(1)}, u32[]{:S(2)}, u32[]{:S(2)}) collective-permute-start(bf16[2,32,256]{2,1,0:T(8,128)(2,1)S(1)} %pad_maximum_fusion.8), channel_id=1, source_target_pairs={{0,4},{4,0},{1,5},{5,1},{2,6},{6,2},{3,7},{7,3},{8,12},{12,8},{9,1... | collective-permute-start | bytes 98312 | tf_op jit(solution)/shard_map/ppermute | solution.py:24
  (2 other events, 9.8 us)

commit v2 on v1

--- a/solution.py
+++ b/solution.py
@@ -127,11 +127,12 @@
 
 
 def forward_products(level, plan, arrived, held, rest, p_in, p_out, sent, spare, sem):
+    x = lax.axis_index("x")
     p_out[...] = p_in[...]
     for r in range(2):
 
         def use(n, block, r=r):
-            p_out[r] += times_transposed(arrived[n], block)
+            p_out[r] += times_transposed(arrived[n if level == 1 else block_column(x, n)], block)
 
         at = BOUNDS + r * LEVELS + level - 1
         use_blocks(plan, r, plan[at], plan[at + 1], held, rest, spare, sem, use)
@@ -218,9 +219,13 @@
     for level in range(1, LEVELS):
         f_r = jnp.where(is_own, f_own, f_par)
         sent = jnp.where(level_r == level - 1, f_r, zero)
-        got = lax.all_to_all(jnp.broadcast_to(sent[None], (NZ, half, width)), "z", 0, 0)
-        got = lax.dynamic_index_in_dim(got.reshape(HZ, 2, half, width), y // 2, 1, keepdims=False)
-        parts = [got] + [lax.ppermute(got, "x", pairs(NX, s)) for s in (1, 2, 3)]
+        if level == 1:
+            got = lax.all_to_all(jnp.broadcast_to(sent[None], (NZ, half, width)), "z", 0, 0)
+            got = lax.dynamic_index_in_dim(got.reshape(HZ, 2, half, width), y // 2, 1, keepdims=False)
+            parts = [got] + [lax.ppermute(got, "x", pairs(NX, s)) for s in (1, 2, 3)]
+        else:
+            got = lax.all_to_all(jnp.broadcast_to(sent[None], (NX * NZ, half, width)), ("x", "z"), 0, 0)
+            parts = [lax.dynamic_index_in_dim(got.reshape(n_j, 2, half, width), y // 2, 1, keepdims=False)]
         if level == 1:
             plan, held, rest, got = pl.pallas_call(
                 prepare,

time: 175 us -> 175 us (level)
  blocking collectives: 68.9 us -> 87.1 us
  starting transfers between devices: 59.8 us -> 50.3 us
  waiting for transfers between devices: 31.4 us -> 23.9 us
    all_to_all x2, blocking collectives: 20.6 us -> 35.2 us  [shards(): lax.all_to_all(jnp.broadcast_to(sent[None], (NX * NZ, half, width)), ('x'...]
    ppermute x9 -> x3, starting transfers between devices: 9.76 us -> 3.25 us  [shards(): parts = [got] + [lax.ppermute(got, 'x', pairs(NX, s)) for s in (1, 2, 3)]]
    ppermute x9 -> x3, waiting for transfers between devices: 6.28 us -> 0.81 us  [shards(): parts = [got] + [lax.ppermute(got, 'x', pairs(NX, s)) for s in (1, 2, 3)]]
    all_to_all x3, blocking collectives: 48.3 us -> 51.9 us  [shards(): arrived = lax.all_to_all(sent, ('x', 'z'), 0, 0)]
    ppermute x5, starting transfers between devices: 23.8 us -> 20.7 us  [swap(): return lax.ppermute(v, 'k', [(0, 1), (1, 0)])]
  transfers between devices with their start and end apart: 33 -> 27, of which waited for: 22 -> 15; matrix products, arithmetic and copies ran while one was open for 1% -> 1% of each run, Pallas kernels for 3% -> 2%
where the time goes in v2:
time: 175 us; the launch traced here: 173 us
  blocking collectives  87.1 us (50%)
  starting transfers between devices  50.3 us (29%)
  waiting for transfers between devices  23.9 us (14%)
  Pallas kernels  7.38 us (4%)
  matrix products  1.97 us (1%)
    all_to_all x3, blocking collectives, shards(): arrived = lax.all_to_all(sent, ('x', 'z'), 0, 0)  51.9 us
    all_to_all x2, blocking collectives, shards(): lax.all_to_all(jnp.broadcast_to(sent[None], (NX * NZ, half, width)), ('x'...  35.2 us
    ppermute x5, starting transfers between devices, swap(): return lax.ppermute(v, 'k', [(0, 1), (1, 0)])  20.7 us
    ppermute x9, starting transfers between devices, shards(): lax.ppermute(rows, 'y', pairs(NY, s)).astype(F32)  10 us
    ppermute x9, starting transfers between devices, shards(): lax.ppermute(o_r, 'y', pairs(NY, s))  9.8 us
    ppermute x9, waiting for transfers between devices, shards(): lax.ppermute(rows, 'y', pairs(NY, s)).astype(F32)  7.89 us
    all_to_all x1, waiting for transfers between devices, shards(): lax.all_to_all(jnp.broadcast_to(sent[None], (NZ, half, width)), 'z', 0, 0)  7.84 us
    ppermute x9, waiting for transfers between devices, shards(): lax.ppermute(o_r, 'y', pairs(NY, s))  6.46 us
  transfers between devices with their start and end apart: 27, of which 15 were waited for; matrix products, arithmetic and copies ran while one was open for 1% of the time, Pallas kernels for 2%

profile of v2, /device:TPU:1, one launch (start us, length us, event | category | flops | bytes accessed | tf_op | source)
XLA Modules:
  0.0 173.5 jit_solution(9551818644928762447)
XLA Ops:
  0.6 3.3 %collective-permute-start = (bf16[256,256]{1,0:T(8,128)(2,1)}, bf16[256,256]{1,0:T(8,128)(2,1)S(1)}, u32[]{:S(2)}, u32[]{:S(2)}) collective-permute-start(bf16[256,256]{1,0:T(8,128)(2,1)} %bitcast.125), channel_id=1, source_target_pairs={{0,4},{4,0},{1,5},{5,1},{2,6},{6,2},{3,7},{7,3},{8,12},{12,8},{9,1... | collective-permute-start | bytes 393224 | tf_op jit(solution)/shard_map/ppermute | solution.py:24
  4.5 1.1 shard_map.68
  6.7 6.5 %all-to-all-start = ((bf16[8,32,256]{2,1,0:T(8,128)(2,1)}), bf16[8,32,256]{2,1,0:T(8,128)(2,1)S(1)}, u32[]{:S(2)}, u32[]{:S(2)}) async-start(bf16[8,32,256]{2,1,0:T(8,128)(2,1)} %broadcast_in_dim.11), calls=%async_computation | async-start | bytes 262144 | tf_op jit(solution)/shard_map/all_to_all | solution.py:223
  13.2 7.8 %all-to-all-done = bf16[8,32,256]{2,1,0:T(8,128)(2,1)S(1)} async-done(((bf16[8,32,256]{2,1,0:T(8,128)(2,1)}), bf16[8,32,256]{2,1,0:T(8,128)(2,1)S(1)}, u32[]{:S(2)}, u32[]{:S(2)}) %all-to-all-start) | async-done | bytes 131104 | tf_op jit(solution)/shard_map/all_to_all | solution.py:223
  21.0 2.5 %collective-permute-start.6 = (bf16[4,32,256]{2,1,0:T(8,128)(2,1)S(1)}, bf16[4,32,256]{2,1,0:T(8,128)(2,1)S(1)}, u32[]{:S(2)}, u32[]{:S(2)}) collective-permute-start(bf16[4,32,256]{2,1,0:T(8,128)(2,1)S(1)} %dynamic-slice_bitcast_fusion.2.here), channel_id=1, source_target_pairs={{0,192},{64,128},{128,64},{192,0},{1,193},{65,129},{129,65},{193,1... | collective-permute-start | bytes 196616 | tf_op jit(solution)/shard_map/ppermute | solution.py:225
  24.3 3.1 %shard_map.69 = (s32[44]{0:T(128)S(4)}, bf16[20,256,256]{2,1,0:T(8,128)(2,1)S(1)}, bf16[12,256,256]{2,1,0:T(8,128)(2,1)}, bf16[4,32,256]{2,1,0:T(8,128)(2,1)S(1)}) custom-call(s32[64]{0:T(128)} %levels_hbm.3, s32[16]{0:T(128)} %bitcast.149, s32[16]{0:T(128)S(1)} %collective-permute-done.2.pattern_par, bf16[16,256,256]{2,1,0:T(8,128)(2,1)} %bitcast.128, ...), custom_call_target="tpu_custom_call" | custom-call | tf_op jit(solution)/shard_map/pallas_call | solution.py:230
  28.3 1.6 shard_map.70
  29.8 1.7 collective-permute-start.9
  32.1 1.1 collective-permute-start.7
  33.9 1.9 %collective-permute-done.8 = bf16[2,32,256]{2,1,0:T(8,128)(2,1)S(1)} collective-permute-done((bf16[2,32,256]{2,1,0:T(8,128)(2,1)S(1)}, bf16[2,32,256]{2,1,0:T(8,128)(2,1)S(1)}, u32[]{:S(2)}, u32[]{:S(2)}) %collective-permute-start.8) | collective-permute-done | bytes 32800 | tf_op jit(solution)/shard_map/ppermute | solution.py:260
  36.3 15.8 %all_to_all.30 = bf16[32,32,256]{2,1,0:T(8,128)(2,1)S(1)} all-to-all(bf16[32,32,256]{2,1,0:T(8,128)(2,1)S(1)} %broadcast_in_dim.13), channel_id=1, replica_groups=mesh['x'=4,'z'=8,'k'=2,'y'=4] {'x','z'}, dimensions={0} | all-to-all | bytes 1048576 | tf_op jit(solution)/shard_map/all_to_all | solution.py:227
  53.8 1.7 collective-permute-start.10
  55.5 1.0 collective-permute-done.12
  57.9 19.4 %all_to_all.31 = bf16[32,32,256]{2,1,0:T(8,128)(2,1)S(1)} all-to-all(bf16[32,32,256]{2,1,0:T(8,128)(2,1)S(1)} %broadcast_in_dim.28), channel_id=1, replica_groups=mesh['x'=4,'z'=8,'k'=2,'y'=4] {'x','z'}, dimensions={0} | all-to-all | bytes 1048576 | tf_op jit(solution)/shard_map/all_to_all | solution.py:227
  77.3 2.1 %collective-permute-start.15 = (bf16[2,32,256]{2,1,0:T(8,128)(2,1)S(1)}, bf16[2,32,256]{2,1,0:T(8,128)(2,1)S(1)}, u32[]{:S(2)}, u32[]{:S(2)}) collective-permute-start(bf16[2,32,256]{2,1,0:T(8,128)(2,1)S(1)} %get-tuple-element.41), channel_id=1, source_target_pairs={{0,3},{1,2},{2,1},{3,0},{4,7},{5,6},{6,5},{7,4},{8,11},{9,10},{10,... | collective-permute-start | bytes 98312 | tf_op jit(solution)/shard_map/ppermute | solution.py:260
  80.7 1.0 collective-permute-done.15
  81.7 2.3 %collective-permute-done.14 = bf16[2,32,256]{2,1,0:T(8,128)(2,1)S(1)} collective-permute-done((bf16[2,32,256]{2,1,0:T(8,128)(2,1)S(1)}, bf16[2,32,256]{2,1,0:T(8,128)(2,1)S(1)}, u32[]{:S(2)}, u32[]{:S(2)}) %collective-permute-start.14) | collective-permute-done | bytes 32800 | tf_op jit(solution)/shard_map/ppermute | solution.py:260
  84.8 18.4 %all_to_all.32 = bf16[32,32,256]{2,1,0:T(8,128)(2,1)S(1)} all-to-all(bf16[32,32,256]{2,1,0:T(8,128)(2,1)S(1)} %shard_map.73), channel_id=1, replica_groups=mesh['x'=4,'z'=8,'k'=2,'y'=4] {'x','z'}, dimensions={0} | all-to-all | bytes 1048576 | tf_op jit(solution)/shard_map/all_to_all | solution.py:283
  103.4 1.2 collective-permute-start.18
  104.7 2.0 %collective-permute-start.16 = (bf16[32,256]{1,0:T(8,128)(2,1)S(1)}, bf16[32,256]{1,0:T(8,128)(2,1)S(1)}, u32[]{:S(2)}, u32[]{:S(2)}) collective-permute-start(bf16[32,256]{1,0:T(8,128)(2,1)S(1)} %convolution_convert_fusion.2), channel_id=1, source_target_pairs={{0,1},{1,0},{2,3},{3,2},{4,5},{5,4},{6,7},{7,6},{8,9},{9,8},{10,11... | collective-permute-start | bytes 49160 | tf_op jit(solution)/shard_map/ppermute | solution.py:286
  107.5 1.5 collective-permute-done.17
  109.2 17.6 %all_to_all.33 = bf16[32,32,256]{2,1,0:T(8,128)(2,1)S(1)} all-to-all(bf16[32,32,256]{2,1,0:T(8,128)(2,1)S(1)} %shard_map.74), channel_id=1, replica_groups=mesh['x'=4,'z'=8,'k'=2,'y'=4] {'x','z'}, dimensions={0} | all-to-all | bytes 1048576 | tf_op jit(solution)/shard_map/all_to_all | solution.py:283
  127.0 1.0 collective-permute-start.21
  128.0 1.0 collective-permute-start.20
  129.0 1.3 collective-permute-start.19
  130.8 1.4 collective-permute-done.20
  132.3 1.3 shard_map.75
  133.6 16.0 %all_to_all.34 = bf16[32,32,256]{2,1,0:T(8,128)(2,1)S(1)} all-to-all(bf16[32,32,256]{2,1,0:T(8,128)(2,1)S(1)} %shard_map.75), channel_id=1, replica_groups=mesh['x'=4,'z'=8,'k'=2,'y'=4] {'x','z'}, dimensions={0} | all-to-all | bytes 1048576 | tf_op jit(solution)/shard_map/all_to_all | solution.py:283
  149.8 1.3 collective-permute-start.24
  151.9 1.1 collective-permute-start.22
  153.6 1.6 collective-permute-done.23
  155.2 16.7 %collective-permute-start.25 = (bf16[2,32,256]{2,1,0:T(8,128)(2,1)S(1)}, bf16[2,32,256]{2,1,0:T(8,128)(2,1)S(1)}, u32[]{:S(2)}, u32[]{:S(2)}) collective-permute-start(bf16[2,32,256]{2,1,0:T(8,128)(2,1)S(1)} %pad_maximum_fusion.6), channel_id=1, source_target_pairs={{0,4},{4,0},{1,5},{5,1},{2,6},{6,2},{3,7},{7,3},{8,12},{12,8},{9,1... | collective-permute-start | bytes 98312 | tf_op jit(solution)/shard_map/ppermute | solution.py:24
  (75 shorter events, 15.2 us)
Async XLA Ops:
  0.6 5.0 %collective-permute-start = (bf16[256,256]{1,0:T(8,128)(2,1)}, bf16[256,256]{1,0:T(8,128)(2,1)S(1)}, u32[]{:S(2)}, u32[]{:S(2)}) collective-permute-start(bf16[256,256]{1,0:T(8,128)(2,1)} %bitcast.125), channel_id=1, source_target_pairs={{0,4},{4,0},{1,5},{5,1},{2,6},{6,2},{3,7},{7,3},{8,12},{12,8},{9,1... | collective-permute-start | bytes 393224 | tf_op jit(solution)/shard_map/ppermute | solution.py:24
  4.0 1.7 collective-permute-start.1
  4.1 1.6 collective-permute-start.2
  5.6 18.6 %collective-permute-start.3 = (bf16[16,256,256]{2,1,0:T(8,128)(2,1)}, bf16[16,256,256]{2,1,0:T(8,128)(2,1)}, u32[]{:S(2)}, u32[]{:S(2)}) collective-permute-start(bf16[16,256,256]{2,1,0:T(8,128)(2,1)} %bitcast.127), channel_id=1, source_target_pairs={{0,4},{4,0},{1,5},{5,1},{2,6},{6,2},{3,7},{7,3},{8,12},{12,8},{9,1... | collective-permute-start | bytes 6291464 | tf_op jit(solution)/shard_map/ppermute | solution.py:24
  6.7 14.3 %all-to-all-start = ((bf16[8,32,256]{2,1,0:T(8,128)(2,1)}), bf16[8,32,256]{2,1,0:T(8,128)(2,1)S(1)}, u32[]{:S(2)}, u32[]{:S(2)}) async-start(bf16[8,32,256]{2,1,0:T(8,128)(2,1)} %broadcast_in_dim.11), calls=%async_computation | async-start | bytes 262144 | tf_op jit(solution)/shard_map/all_to_all | solution.py:223
  21.0 6.4 %collective-permute-start.6 = (bf16[4,32,256]{2,1,0:T(8,128)(2,1)S(1)}, bf16[4,32,256]{2,1,0:T(8,128)(2,1)S(1)}, u32[]{:S(2)}, u32[]{:S(2)}) collective-permute-start(bf16[4,32,256]{2,1,0:T(8,128)(2,1)S(1)} %dynamic-slice_bitcast_fusion.2.here), channel_id=1, source_target_pairs={{0,192},{64,128},{128,64},{192,0},{1,193},{65,129},{129,65},{193,1... | collective-permute-start | bytes 196616 | tf_op jit(solution)/shard_map/ppermute | solution.py:225
  23.5 4.7 %collective-permute-start.5 = (bf16[4,32,256]{2,1,0:T(8,128)(2,1)S(1)}, bf16[4,32,256]{2,1,0:T(8,128)(2,1)S(1)}, u32[]{:S(2)}, u32[]{:S(2)}) collective-permute-start(bf16[4,32,256]{2,1,0:T(8,128)(2,1)S(1)} %dynamic-slice_bitcast_fusion.2.here), channel_id=1, source_target_pairs={{0,128},{64,192},{128,0},{192,64},{1,129},{65,193},{129,1},{193,65... | collective-permute-start | bytes 196616 | tf_op jit(solution)/shard_map/ppermute | solution.py:225
  24.0 4.2 %collective-permute-start.4 = (bf16[4,32,256]{2,1,0:T(8,128)(2,1)S(1)}, bf16[4,32,256]{2,1,0:T(8,128)(2,1)S(1)}, u32[]{:S(2)}, u32[]{:S(2)}) collective-permute-start(bf16[4,32,256]{2,1,0:T(8,128)(2,1)S(1)} %dynamic-slice_bitcast_fusion.2.here), channel_id=1, source_target_pairs={{0,64},{64,0},{128,192},{192,128},{1,65},{65,1},{129,193},{193,129... | collective-permute-start | bytes 196616 | tf_op jit(solution)/shard_map/ppermute | solution.py:225
  28.3 7.7 %copy-start = (bf16[1,256,256]{2,1,0:T(8,128)(2,1)S(1)}, bf16[1,256,256]{2,1,0:T(8,128)(2,1)}, u32[]{:S(2)}) copy-start(bf16[1,256,256]{2,1,0:T(8,128)(2,1)} %param.6) | copy-start | bytes 393220
  29.8 4.1 %collective-permute-start.9 = (bf16[2,32,256]{2,1,0:T(8,128)(2,1)S(1)}, bf16[2,32,256]{2,1,0:T(8,128)(2,1)S(1)}, u32[]{:S(2)}, u32[]{:S(2)}) collective-permute-start(bf16[2,32,256]{2,1,0:T(8,128)(2,1)S(1)} %get-tuple-element.37), channel_id=1, source_target_pairs={{0,3},{1,2},{2,1},{3,0},{4,7},{5,6},{6,5},{7,4},{8,11},{9,10},{10,... | collective-permute-start | bytes 98312 | tf_op jit(solution)/shard_map/ppermute | solution.py:260
  31.5 4.3 %collective-permute-start.8 = (bf16[2,32,256]{2,1,0:T(8,128)(2,1)S(1)}, bf16[2,32,256]{2,1,0:T(8,128)(2,1)S(1)}, u32[]{:S(2)}, u32[]{:S(2)}) collective-permute-start(bf16[2,32,256]{2,1,0:T(8,128)(2,1)S(1)} %get-tuple-element.37), channel_id=1, source_target_pairs={{0,2},{1,3},{2,0},{3,1},{4,6},{5,7},{6,4},{7,5},{8,10},{9,11},{10,... | collective-permute-start | bytes 98312 | tf_op jit(solution)/shard_map/ppermute | solution.py:260
  32.1 3.7 %collective-permute-start.7 = (bf16[2,32,256]{2,1,0:T(8,128)(2,1)S(1)}, bf16[2,32,256]{2,1,0:T(8,128)(2,1)S(1)}, u32[]{:S(2)}, u32[]{:S(2)}) collective-permute-start(bf16[2,32,256]{2,1,0:T(8,128)(2,1)S(1)} %get-tuple-element.37), channel_id=1, source_target_pairs={{0,1},{1,0},{2,3},{3,2},{4,5},{5,4},{6,7},{7,6},{8,9},{9,8},{10,11... | collective-permute-start | bytes 98312 | tf_op jit(solution)/shard_map/ppermute | solution.py:260
  52.1 4.4 %collective-permute-start.12 = (bf16[2,32,256]{2,1,0:T(8,128)(2,1)S(1)}, bf16[2,32,256]{2,1,0:T(8,128)(2,1)S(1)}, u32[]{:S(2)}, u32[]{:S(2)}) collective-permute-start(bf16[2,32,256]{2,1,0:T(8,128)(2,1)S(1)} %get-tuple-element.39), channel_id=1, source_target_pairs={{0,3},{1,2},{2,1},{3,0},{4,7},{5,6},{6,5},{7,4},{8,11},{9,10},{10,... | collective-permute-start | bytes 98312 | tf_op jit(solution)/shard_map/ppermute | solution.py:260
  52.9 4.6 %collective-permute-start.11 = (bf16[2,32,256]{2,1,0:T(8,128)(2,1)S(1)}, bf16[2,32,256]{2,1,0:T(8,128)(2,1)S(1)}, u32[]{:S(2)}, u32[]{:S(2)}) collective-permute-start(bf16[2,32,256]{2,1,0:T(8,128)(2,1)S(1)} %get-tuple-element.39), channel_id=1, source_target_pairs={{0,2},{1,3},{2,0},{3,1},{4,6},{5,7},{6,4},{7,5},{8,10},{9,11},{10,... | collective-permute-start | bytes 98312 | tf_op jit(solution)/shard_map/ppermute | solution.py:260
  53.8 3.7 %collective-permute-start.10 = (bf16[2,32,256]{2,1,0:T(8,128)(2,1)S(1)}, bf16[2,32,256]{2,1,0:T(8,128)(2,1)S(1)}, u32[]{:S(2)}, u32[]{:S(2)}) collective-permute-start(bf16[2,32,256]{2,1,0:T(8,128)(2,1)S(1)} %get-tuple-element.39), channel_id=1, source_target_pairs={{0,1},{1,0},{2,3},{3,2},{4,5},{5,4},{6,7},{7,6},{8,9},{9,8},{10,11... | collective-permute-start | bytes 98312 | tf_op jit(solution)/shard_map/ppermute | solution.py:260
  77.3 4.4 %collective-permute-start.15 = (bf16[2,32,256]{2,1,0:T(8,128)(2,1)S(1)}, bf16[2,32,256]{2,1,0:T(8,128)(2,1)S(1)}, u32[]{:S(2)}, u32[]{:S(2)}) collective-permute-start(bf16[2,32,256]{2,1,0:T(8,128)(2,1)S(1)} %get-tuple-element.41), channel_id=1, source_target_pairs={{0,3},{1,2},{2,1},{3,0},{4,7},{5,6},{6,5},{7,4},{8,11},{9,10},{10,... | collective-permute-start | bytes 98312 | tf_op jit(solution)/shard_map/ppermute | solution.py:260
  79.5 4.6 %collective-permute-start.14 = (bf16[2,32,256]{2,1,0:T(8,128)(2,1)S(1)}, bf16[2,32,256]{2,1,0:T(8,128)(2,1)S(1)}, u32[]{:S(2)}, u32[]{:S(2)}) collective-permute-start(bf16[2,32,256]{2,1,0:T(8,128)(2,1)S(1)} %get-tuple-element.41), channel_id=1, source_target_pairs={{0,2},{1,3},{2,0},{3,1},{4,6},{5,7},{6,4},{7,5},{8,10},{9,11},{10,... | collective-permute-start | bytes 98312 | tf_op jit(solution)/shard_map/ppermute | solution.py:260
  80.2 3.8 %collective-permute-start.13 = (bf16[2,32,256]{2,1,0:T(8,128)(2,1)S(1)}, bf16[2,32,256]{2,1,0:T(8,128)(2,1)S(1)}, u32[]{:S(2)}, u32[]{:S(2)}) collective-permute-start(bf16[2,32,256]{2,1,0:T(8,128)(2,1)S(1)} %get-tuple-element.41), channel_id=1, source_target_pairs={{0,1},{1,0},{2,3},{3,2},{4,5},{5,4},{6,7},{7,6},{8,9},{9,8},{10,11... | collective-permute-start | bytes 98312 | tf_op jit(solution)/shard_map/ppermute | solution.py:260
  103.4 4.1 %collective-permute-start.18 = (bf16[32,256]{1,0:T(8,128)(2,1)S(1)}, bf16[32,256]{1,0:T(8,128)(2,1)S(1)}, u32[]{:S(2)}, u32[]{:S(2)}) collective-permute-start(bf16[32,256]{1,0:T(8,128)(2,1)S(1)} %convolution_convert_fusion.2), channel_id=1, source_target_pairs={{0,3},{1,2},{2,1},{3,0},{4,7},{5,6},{6,5},{7,4},{8,11},{9,10},{10,... | collective-permute-start | bytes 49160 | tf_op jit(solution)/shard_map/ppermute | solution.py:286
  104.7 4.4 %collective-permute-start.17 = (bf16[32,256]{1,0:T(8,128)(2,1)S(1)}, bf16[32,256]{1,0:T(8,128)(2,1)S(1)}, u32[]{:S(2)}, u32[]{:S(2)}) collective-permute-start(bf16[32,256]{1,0:T(8,128)(2,1)S(1)} %convolution_convert_fusion.2), channel_id=1, source_target_pairs={{0,2},{1,3},{2,0},{3,1},{4,6},{5,7},{6,4},{7,5},{8,10},{9,11},{10,... | collective-permute-start | bytes 49160 | tf_op jit(solution)/shard_map/ppermute | solution.py:286
  104.7 4.4 %collective-permute-start.16 = (bf16[32,256]{1,0:T(8,128)(2,1)S(1)}, bf16[32,256]{1,0:T(8,128)(2,1)S(1)}, u32[]{:S(2)}, u32[]{:S(2)}) collective-permute-start(bf16[32,256]{1,0:T(8,128)(2,1)S(1)} %convolution_convert_fusion.2), channel_id=1, source_target_pairs={{0,1},{1,0},{2,3},{3,2},{4,5},{5,4},{6,7},{7,6},{8,9},{9,8},{10,11... | collective-permute-start | bytes 49160 | tf_op jit(solution)/shard_map/ppermute | solution.py:286
  127.0 3.8 %collective-permute-start.21 = (bf16[32,256]{1,0:T(8,128)(2,1)S(1)}, bf16[32,256]{1,0:T(8,128)(2,1)S(1)}, u32[]{:S(2)}, u32[]{:S(2)}) collective-permute-start(bf16[32,256]{1,0:T(8,128)(2,1)S(1)} %convolution_convert_fusion.1), channel_id=1, source_target_pairs={{0,3},{1,2},{2,1},{3,0},{4,7},{5,6},{6,5},{7,4},{8,11},{9,10},{10,... | collective-permute-start | bytes 49160 | tf_op jit(solution)/shard_map/ppermute | solution.py:286
  128.0 4.2 %collective-permute-start.20 = (bf16[32,256]{1,0:T(8,128)(2,1)S(1)}, bf16[32,256]{1,0:T(8,128)(2,1)S(1)}, u32[]{:S(2)}, u32[]{:S(2)}) collective-permute-start(bf16[32,256]{1,0:T(8,128)(2,1)S(1)} %convolution_convert_fusion.1), channel_id=1, source_target_pairs={{0,2},{1,3},{2,0},{3,1},{4,6},{5,7},{6,4},{7,5},{8,10},{9,11},{10,... | collective-permute-start | bytes 49160 | tf_op jit(solution)/shard_map/ppermute | solution.py:286
  129.0 3.2 %collective-permute-start.19 = (bf16[32,256]{1,0:T(8,128)(2,1)S(1)}, bf16[32,256]{1,0:T(8,128)(2,1)S(1)}, u32[]{:S(2)}, u32[]{:S(2)}) collective-permute-start(bf16[32,256]{1,0:T(8,128)(2,1)S(1)} %convolution_convert_fusion.1), channel_id=1, source_target_pairs={{0,1},{1,0},{2,3},{3,2},{4,5},{5,4},{6,7},{7,6},{8,9},{9,8},{10,11... | collective-permute-start | bytes 49160 | tf_op jit(solution)/shard_map/ppermute | solution.py:286
  149.8 3.8 %collective-permute-start.24 = (bf16[32,256]{1,0:T(8,128)(2,1)S(1)}, bf16[32,256]{1,0:T(8,128)(2,1)S(1)}, u32[]{:S(2)}, u32[]{:S(2)}) collective-permute-start(bf16[32,256]{1,0:T(8,128)(2,1)S(1)} %convolution_convert_fusion), channel_id=1, source_target_pairs={{0,3},{1,2},{2,1},{3,0},{4,7},{5,6},{6,5},{7,4},{8,11},{9,10},{10,... | collective-permute-start | bytes 49160 | tf_op jit(solution)/shard_map/ppermute | solution.py:286
  151.1 4.1 %collective-permute-start.23 = (bf16[32,256]{1,0:T(8,128)(2,1)S(1)}, bf16[32,256]{1,0:T(8,128)(2,1)S(1)}, u32[]{:S(2)}, u32[]{:S(2)}) collective-permute-start(bf16[32,256]{1,0:T(8,128)(2,1)S(1)} %convolution_convert_fusion), channel_id=1, source_target_pairs={{0,2},{1,3},{2,0},{3,1},{4,6},{5,7},{6,4},{7,5},{8,10},{9,11},{10,... | collective-permute-start | bytes 49160 | tf_op jit(solution)/shard_map/ppermute | solution.py:286
  151.9 3.2 %collective-permute-start.22 = (bf16[32,256]{1,0:T(8,128)(2,1)S(1)}, bf16[32,256]{1,0:T(8,128)(2,1)S(1)}, u32[]{:S(2)}, u32[]{:S(2)}) collective-permute-start(bf16[32,256]{1,0:T(8,128)(2,1)S(1)} %convolution_convert_fusion), channel_id=1, source_target_pairs={{0,1},{1,0},{2,3},{3,2},{4,5},{5,4},{6,7},{7,6},{8,9},{9,8},{10,11... | collective-permute-start | bytes 49160 | tf_op jit(solution)/shard_map/ppermute | solution.py:286
  155.2 17.6 %collective-permute-start.25 = (bf16[2,32,256]{2,1,0:T(8,128)(2,1)S(1)}, bf16[2,32,256]{2,1,0:T(8,128)(2,1)S(1)}, u32[]{:S(2)}, u32[]{:S(2)}) collective-permute-start(bf16[2,32,256]{2,1,0:T(8,128)(2,1)S(1)} %pad_maximum_fusion.6), channel_id=1, source_target_pairs={{0,4},{4,0},{1,5},{5,1},{2,6},{6,2},{3,7},{7,3},{8,12},{12,8},{9,1... | collective-permute-start | bytes 98312 | tf_op jit(solution)/shard_map/ppermute | solution.py:24

commit v3 on v2

--- a/solution.py
+++ b/solution.py
@@ -257,7 +257,7 @@
             scratch_shapes=fetch,
             compiler_params=params,
         )(plan, jnp.concatenate(parts), held, rest, sums)
-        others = [lax.ppermute(rows, "y", pairs(NY, s)).astype(F32) for s in (1, 2, 3)]
+        others = [lax.ppermute(rows, "y", pairs(NY, s)).astype(F32) for s in (1, 3, 2)]
         other = others[0] + others[1] + others[2]
         s_own = sums[0] + jnp.where(k == 0, other[0], other[1])
         s_par = sums[1] + jnp.where(k == 0, other[1], other[0])

time: 175 us -> 175 us (level)
    all_to_all x3, blocking collectives: 51.9 us -> 53.8 us  [shards(): arrived = lax.all_to_all(sent, ('x', 'z'), 0, 0)]
where the time goes in v3:
time: 175 us; the launch traced here: 174 us
  blocking collectives  88.1 us (50%)
  starting transfers between devices  50 us (29%)
  waiting for transfers between devices  25.5 us (15%)
  Pallas kernels  5.81 us (3%)
  matrix products  1.97 us (1%)
    all_to_all x3, blocking collectives, shards(): arrived = lax.all_to_all(sent, ('x', 'z'), 0, 0)  53.8 us
    all_to_all x2, blocking collectives, shards(): lax.all_to_all(jnp.broadcast_to(sent[None], (NX * NZ, half, width)), ('x'...  34.3 us
    ppermute x5, starting transfers between devices, swap(): return lax.ppermute(v, 'k', [(0, 1), (1, 0)])  21.5 us
    ppermute x9, starting transfers between devices, shards(): lax.ppermute(o_r, 'y', pairs(NY, s))  9.8 us
    ppermute x9, waiting for transfers between devices, shards(): lax.ppermute(rows, 'y', pairs(NY, s)).astype(F32)  9.33 us
    ppermute x9, starting transfers between devices, shards(): lax.ppermute(rows, 'y', pairs(NY, s)).astype(F32)  8.99 us
    all_to_all x1, waiting for transfers between devices, shards(): lax.all_to_all(jnp.broadcast_to(sent[None], (NZ, half, width)), 'z', 0, 0)  7.84 us
    ppermute x9, waiting for transfers between devices, shards(): lax.ppermute(o_r, 'y', pairs(NY, s))  6.48 us
  transfers between devices with their start and end apart: 27, of which 15 were waited for; matrix products, arithmetic and copies ran while one was open for 1% of the time, Pallas kernels for 2%

profile of v3, /device:TPU:1, one launch (start us, length us, event | category | flops | bytes accessed | tf_op | source)
XLA Modules:
  0.0 174.3 jit_solution(7417359674642284817)
XLA Ops:
  0.6 3.3 %collective-permute-start = (bf16[256,256]{1,0:T(8,128)(2,1)}, bf16[256,256]{1,0:T(8,128)(2,1)S(1)}, u32[]{:S(2)}, u32[]{:S(2)}) collective-permute-start(bf16[256,256]{1,0:T(8,128)(2,1)} %bitcast.125), channel_id=1, source_target_pairs={{0,4},{4,0},{1,5},{5,1},{2,6},{6,2},{3,7},{7,3},{8,12},{12,8},{9,1... | collective-permute-start | bytes 393224 | tf_op jit(solution)/shard_map/ppermute | solution.py:24
  4.5 1.1 shard_map.68
  6.7 6.5 %all-to-all-start = ((bf16[8,32,256]{2,1,0:T(8,128)(2,1)}), bf16[8,32,256]{2,1,0:T(8,128)(2,1)S(1)}, u32[]{:S(2)}, u32[]{:S(2)}) async-start(bf16[8,32,256]{2,1,0:T(8,128)(2,1)} %broadcast_in_dim.11), calls=%async_computation | async-start | bytes 262144 | tf_op jit(solution)/shard_map/all_to_all | solution.py:223
  13.2 7.8 %all-to-all-done = bf16[8,32,256]{2,1,0:T(8,128)(2,1)S(1)} async-done(((bf16[8,32,256]{2,1,0:T(8,128)(2,1)}), bf16[8,32,256]{2,1,0:T(8,128)(2,1)S(1)}, u32[]{:S(2)}, u32[]{:S(2)}) %all-to-all-start) | async-done | bytes 131104 | tf_op jit(solution)/shard_map/all_to_all | solution.py:223
  21.0 2.5 %collective-permute-start.6 = (bf16[4,32,256]{2,1,0:T(8,128)(2,1)S(1)}, bf16[4,32,256]{2,1,0:T(8,128)(2,1)S(1)}, u32[]{:S(2)}, u32[]{:S(2)}) collective-permute-start(bf16[4,32,256]{2,1,0:T(8,128)(2,1)S(1)} %dynamic-slice_bitcast_fusion.2.here), channel_id=1, source_target_pairs={{0,192},{64,128},{128,64},{192,0},{1,193},{65,129},{129,65},{193,1... | collective-permute-start | bytes 196616 | tf_op jit(solution)/shard_map/ppermute | solution.py:225
  24.3 2.9 %shard_map.69 = (s32[44]{0:T(128)S(4)}, bf16[20,256,256]{2,1,0:T(8,128)(2,1)S(1)}, bf16[12,256,256]{2,1,0:T(8,128)(2,1)}, bf16[4,32,256]{2,1,0:T(8,128)(2,1)S(1)}) custom-call(s32[64]{0:T(128)} %levels_hbm.3, s32[16]{0:T(128)} %bitcast.149, s32[16]{0:T(128)S(1)} %collective-permute-done.2.pattern_par, bf16[16,256,256]{2,1,0:T(8,128)(2,1)} %bitcast.128, ...), custom_call_target="tpu_custom_call" | custom-call | tf_op jit(solution)/shard_map/pallas_call | solution.py:230
  27.2 1.0 collective-permute-done.5
  29.1 2.8 %collective-permute-start.9 = (bf16[2,32,256]{2,1,0:T(8,128)(2,1)S(1)}, bf16[2,32,256]{2,1,0:T(8,128)(2,1)S(1)}, u32[]{:S(2)}, u32[]{:S(2)}) collective-permute-start(bf16[2,32,256]{2,1,0:T(8,128)(2,1)S(1)} %get-tuple-element.37), channel_id=1, source_target_pairs={{0,2},{1,3},{2,0},{3,1},{4,6},{5,7},{6,4},{7,5},{8,10},{9,11},{10,... | collective-permute-start | bytes 98312 | tf_op jit(solution)/shard_map/ppermute | solution.py:260
  32.5 1.0 collective-permute-done.9
  33.4 2.4 %collective-permute-done.8 = bf16[2,32,256]{2,1,0:T(8,128)(2,1)S(1)} collective-permute-done((bf16[2,32,256]{2,1,0:T(8,128)(2,1)S(1)}, bf16[2,32,256]{2,1,0:T(8,128)(2,1)S(1)}, u32[]{:S(2)}, u32[]{:S(2)}) %collective-permute-start.8) | collective-permute-done | bytes 32800 | tf_op jit(solution)/shard_map/ppermute | solution.py:260
  36.3 16.2 %all_to_all.30 = bf16[32,32,256]{2,1,0:T(8,128)(2,1)S(1)} all-to-all(bf16[32,32,256]{2,1,0:T(8,128)(2,1)S(1)} %broadcast_in_dim.13), channel_id=1, replica_groups=mesh['x'=4,'z'=8,'k'=2,'y'=4] {'x','z'}, dimensions={0} | all-to-all | bytes 1048576 | tf_op jit(solution)/shard_map/all_to_all | solution.py:227
  52.7 1.3 collective-permute-start.12
  55.4 1.9 %collective-permute-done.12 = bf16[2,32,256]{2,1,0:T(8,128)(2,1)S(1)} collective-permute-done((bf16[2,32,256]{2,1,0:T(8,128)(2,1)S(1)}, bf16[2,32,256]{2,1,0:T(8,128)(2,1)S(1)}, u32[]{:S(2)}, u32[]{:S(2)}) %collective-permute-start.12) | collective-permute-done | bytes 32800 | tf_op jit(solution)/shard_map/ppermute | solution.py:260
  58.7 18.0 %all_to_all.31 = bf16[32,32,256]{2,1,0:T(8,128)(2,1)S(1)} all-to-all(bf16[32,32,256]{2,1,0:T(8,128)(2,1)S(1)} %broadcast_in_dim.28), channel_id=1, replica_groups=mesh['x'=4,'z'=8,'k'=2,'y'=4] {'x','z'}, dimensions={0} | all-to-all | bytes 1048576 | tf_op jit(solution)/shard_map/all_to_all | solution.py:227
  76.7 1.7 %collective-permute-start.15 = (bf16[2,32,256]{2,1,0:T(8,128)(2,1)S(1)}, bf16[2,32,256]{2,1,0:T(8,128)(2,1)S(1)}, u32[]{:S(2)}, u32[]{:S(2)}) collective-permute-start(bf16[2,32,256]{2,1,0:T(8,128)(2,1)S(1)} %get-tuple-element.41), channel_id=1, source_target_pairs={{0,2},{1,3},{2,0},{3,1},{4,6},{5,7},{6,4},{7,5},{8,10},{9,11},{10,... | collective-permute-start | bytes 98312 | tf_op jit(solution)/shard_map/ppermute | solution.py:260
  78.5 1.1 collective-permute-start.14
  79.6 1.8 %collective-permute-done.15 = bf16[2,32,256]{2,1,0:T(8,128)(2,1)S(1)} collective-permute-done((bf16[2,32,256]{2,1,0:T(8,128)(2,1)S(1)}, bf16[2,32,256]{2,1,0:T(8,128)(2,1)S(1)}, u32[]{:S(2)}, u32[]{:S(2)}) %collective-permute-start.15) | collective-permute-done | bytes 32800 | tf_op jit(solution)/shard_map/ppermute | solution.py:260
  81.4 1.4 collective-permute-done.14
  83.6 18.8 %all_to_all.32 = bf16[32,32,256]{2,1,0:T(8,128)(2,1)S(1)} all-to-all(bf16[32,32,256]{2,1,0:T(8,128)(2,1)S(1)} %shard_map.73), channel_id=1, replica_groups=mesh['x'=4,'z'=8,'k'=2,'y'=4] {'x','z'}, dimensions={0} | all-to-all | bytes 1048576 | tf_op jit(solution)/shard_map/all_to_all | solution.py:283
  102.6 1.6 collective-permute-start.18
  104.7 1.2 collective-permute-start.16
  106.7 1.9 %collective-permute-done.17 = bf16[32,256]{1,0:T(8,128)(2,1)S(1)} collective-permute-done((bf16[32,256]{1,0:T(8,128)(2,1)S(1)}, bf16[32,256]{1,0:T(8,128)(2,1)S(1)}, u32[]{:S(2)}, u32[]{:S(2)}) %collective-permute-start.17) | collective-permute-done | bytes 16416 | tf_op jit(solution)/shard_map/ppermute | solution.py:286
  108.7 17.3 %all_to_all.33 = bf16[32,32,256]{2,1,0:T(8,128)(2,1)S(1)} all-to-all(bf16[32,32,256]{2,1,0:T(8,128)(2,1)S(1)} %shard_map.74), channel_id=1, replica_groups=mesh['x'=4,'z'=8,'k'=2,'y'=4] {'x','z'}, dimensions={0} | all-to-all | bytes 1048576 | tf_op jit(solution)/shard_map/all_to_all | solution.py:283
  126.3 1.0 collective-permute-start.21
  127.3 1.0 collective-permute-start.20
  128.2 1.3 collective-permute-start.19
  130.1 1.6 collective-permute-done.20
  132.4 17.7 %all_to_all.34 = bf16[32,32,256]{2,1,0:T(8,128)(2,1)S(1)} all-to-all(bf16[32,32,256]{2,1,0:T(8,128)(2,1)S(1)} %shard_map.75), channel_id=1, replica_groups=mesh['x'=4,'z'=8,'k'=2,'y'=4] {'x','z'}, dimensions={0} | all-to-all | bytes 1048576 | tf_op jit(solution)/shard_map/all_to_all | solution.py:283
  151.2 1.0 collective-permute-start.23
  152.2 1.5 collective-permute-start.22
  154.1 1.1 collective-permute-done.23
  155.3 17.5 %collective-permute-start.25 = (bf16[2,32,256]{2,1,0:T(8,128)(2,1)S(1)}, bf16[2,32,256]{2,1,0:T(8,128)(2,1)S(1)}, u32[]{:S(2)}, u32[]{:S(2)}) collective-permute-start(bf16[2,32,256]{2,1,0:T(8,128)(2,1)S(1)} %pad_maximum_fusion.6), channel_id=1, source_target_pairs={{0,4},{4,0},{1,5},{5,1},{2,6},{6,2},{3,7},{7,3},{8,12},{12,8},{9,1... | collective-permute-start | bytes 98312 | tf_op jit(solution)/shard_map/ppermute | solution.py:24
  (75 shorter events, 14.3 us)
Async XLA Ops:
  0.6 5.0 %collective-permute-start = (bf16[256,256]{1,0:T(8,128)(2,1)}, bf16[256,256]{1,0:T(8,128)(2,1)S(1)}, u32[]{:S(2)}, u32[]{:S(2)}) collective-permute-start(bf16[256,256]{1,0:T(8,128)(2,1)} %bitcast.125), channel_id=1, source_target_pairs={{0,4},{4,0},{1,5},{5,1},{2,6},{6,2},{3,7},{7,3},{8,12},{12,8},{9,1... | collective-permute-start | bytes 393224 | tf_op jit(solution)/shard_map/ppermute | solution.py:24
  4.0 1.7 collective-permute-start.1
  4.1 1.6 collective-permute-start.2
  5.6 18.6 %collective-permute-start.3 = (bf16[16,256,256]{2,1,0:T(8,128)(2,1)}, bf16[16,256,256]{2,1,0:T(8,128)(2,1)}, u32[]{:S(2)}, u32[]{:S(2)}) collective-permute-start(bf16[16,256,256]{2,1,0:T(8,128)(2,1)} %bitcast.127), channel_id=1, source_target_pairs={{0,4},{4,0},{1,5},{5,1},{2,6},{6,2},{3,7},{7,3},{8,12},{12,8},{9,1... | collective-permute-start | bytes 6291464 | tf_op jit(solution)/shard_map/ppermute | solution.py:24
  6.7 14.3 %all-to-all-start = ((bf16[8,32,256]{2,1,0:T(8,128)(2,1)}), bf16[8,32,256]{2,1,0:T(8,128)(2,1)S(1)}, u32[]{:S(2)}, u32[]{:S(2)}) async-start(bf16[8,32,256]{2,1,0:T(8,128)(2,1)} %broadcast_in_dim.11), calls=%async_computation | async-start | bytes 262144 | tf_op jit(solution)/shard_map/all_to_all | solution.py:223
  21.0 6.2 %collective-permute-start.6 = (bf16[4,32,256]{2,1,0:T(8,128)(2,1)S(1)}, bf16[4,32,256]{2,1,0:T(8,128)(2,1)S(1)}, u32[]{:S(2)}, u32[]{:S(2)}) collective-permute-start(bf16[4,32,256]{2,1,0:T(8,128)(2,1)S(1)} %dynamic-slice_bitcast_fusion.2.here), channel_id=1, source_target_pairs={{0,192},{64,128},{128,64},{192,0},{1,193},{65,129},{129,65},{193,1... | collective-permute-start | bytes 196616 | tf_op jit(solution)/shard_map/ppermute | solution.py:225
  23.5 4.7 %collective-permute-start.5 = (bf16[4,32,256]{2,1,0:T(8,128)(2,1)S(1)}, bf16[4,32,256]{2,1,0:T(8,128)(2,1)S(1)}, u32[]{:S(2)}, u32[]{:S(2)}) collective-permute-start(bf16[4,32,256]{2,1,0:T(8,128)(2,1)S(1)} %dynamic-slice_bitcast_fusion.2.here), channel_id=1, source_target_pairs={{0,128},{64,192},{128,0},{192,64},{1,129},{65,193},{129,1},{193,65... | collective-permute-start | bytes 196616 | tf_op jit(solution)/shard_map/ppermute | solution.py:225
  24.0 4.2 %collective-permute-start.4 = (bf16[4,32,256]{2,1,0:T(8,128)(2,1)S(1)}, bf16[4,32,256]{2,1,0:T(8,128)(2,1)S(1)}, u32[]{:S(2)}, u32[]{:S(2)}) collective-permute-start(bf16[4,32,256]{2,1,0:T(8,128)(2,1)S(1)} %dynamic-slice_bitcast_fusion.2.here), channel_id=1, source_target_pairs={{0,64},{64,0},{128,192},{192,128},{1,65},{65,1},{129,193},{193,129... | collective-permute-start | bytes 196616 | tf_op jit(solution)/shard_map/ppermute | solution.py:225
  28.3 7.8 %copy-start = (bf16[1,256,256]{2,1,0:T(8,128)(2,1)S(1)}, bf16[1,256,256]{2,1,0:T(8,128)(2,1)}, u32[]{:S(2)}) copy-start(bf16[1,256,256]{2,1,0:T(8,128)(2,1)} %param.6) | copy-start | bytes 393220
  29.1 4.4 %collective-permute-start.9 = (bf16[2,32,256]{2,1,0:T(8,128)(2,1)S(1)}, bf16[2,32,256]{2,1,0:T(8,128)(2,1)S(1)}, u32[]{:S(2)}, u32[]{:S(2)}) collective-permute-start(bf16[2,32,256]{2,1,0:T(8,128)(2,1)S(1)} %get-tuple-element.37), channel_id=1, source_target_pairs={{0,2},{1,3},{2,0},{3,1},{4,6},{5,7},{6,4},{7,5},{8,10},{9,11},{10,... | collective-permute-start | bytes 98312 | tf_op jit(solution)/shard_map/ppermute | solution.py:260
  31.9 4.0 %collective-permute-start.8 = (bf16[2,32,256]{2,1,0:T(8,128)(2,1)S(1)}, bf16[2,32,256]{2,1,0:T(8,128)(2,1)S(1)}, u32[]{:S(2)}, u32[]{:S(2)}) collective-permute-start(bf16[2,32,256]{2,1,0:T(8,128)(2,1)S(1)} %get-tuple-element.37), channel_id=1, source_target_pairs={{0,3},{1,2},{2,1},{3,0},{4,7},{5,6},{6,5},{7,4},{8,11},{9,10},{10,... | collective-permute-start | bytes 98312 | tf_op jit(solution)/shard_map/ppermute | solution.py:260
  32.5 3.4 %collective-permute-start.7 = (bf16[2,32,256]{2,1,0:T(8,128)(2,1)S(1)}, bf16[2,32,256]{2,1,0:T(8,128)(2,1)S(1)}, u32[]{:S(2)}, u32[]{:S(2)}) collective-permute-start(bf16[2,32,256]{2,1,0:T(8,128)(2,1)S(1)} %get-tuple-element.37), channel_id=1, source_target_pairs={{0,1},{1,0},{2,3},{3,2},{4,5},{5,4},{6,7},{7,6},{8,9},{9,8},{10,11... | collective-permute-start | bytes 98312 | tf_op jit(solution)/shard_map/ppermute | solution.py:260
  52.7 4.7 %collective-permute-start.12 = (bf16[2,32,256]{2,1,0:T(8,128)(2,1)S(1)}, bf16[2,32,256]{2,1,0:T(8,128)(2,1)S(1)}, u32[]{:S(2)}, u32[]{:S(2)}) collective-permute-start(bf16[2,32,256]{2,1,0:T(8,128)(2,1)S(1)} %get-tuple-element.39), channel_id=1, source_target_pairs={{0,2},{1,3},{2,0},{3,1},{4,6},{5,7},{6,4},{7,5},{8,10},{9,11},{10,... | collective-permute-start | bytes 98312 | tf_op jit(solution)/shard_map/ppermute | solution.py:260
  53.9 4.3 %collective-permute-start.11 = (bf16[2,32,256]{2,1,0:T(8,128)(2,1)S(1)}, bf16[2,32,256]{2,1,0:T(8,128)(2,1)S(1)}, u32[]{:S(2)}, u32[]{:S(2)}) collective-permute-start(bf16[2,32,256]{2,1,0:T(8,128)(2,1)S(1)} %get-tuple-element.39), channel_id=1, source_target_pairs={{0,3},{1,2},{2,1},{3,0},{4,7},{5,6},{6,5},{7,4},{8,11},{9,10},{10,... | collective-permute-start | bytes 98312 | tf_op jit(solution)/shard_map/ppermute | solution.py:260
  54.7 3.5 %collective-permute-start.10 = (bf16[2,32,256]{2,1,0:T(8,128)(2,1)S(1)}, bf16[2,32,256]{2,1,0:T(8,128)(2,1)S(1)}, u32[]{:S(2)}, u32[]{:S(2)}) collective-permute-start(bf16[2,32,256]{2,1,0:T(8,128)(2,1)S(1)} %get-tuple-element.39), channel_id=1, source_target_pairs={{0,1},{1,0},{2,3},{3,2},{4,5},{5,4},{6,7},{7,6},{8,9},{9,8},{10,11... | collective-permute-start | bytes 98312 | tf_op jit(solution)/shard_map/ppermute | solution.py:260
  76.7 4.7 %collective-permute-start.15 = (bf16[2,32,256]{2,1,0:T(8,128)(2,1)S(1)}, bf16[2,32,256]{2,1,0:T(8,128)(2,1)S(1)}, u32[]{:S(2)}, u32[]{:S(2)}) collective-permute-start(bf16[2,32,256]{2,1,0:T(8,128)(2,1)S(1)} %get-tuple-element.41), channel_id=1, source_target_pairs={{0,2},{1,3},{2,0},{3,1},{4,6},{5,7},{6,4},{7,5},{8,10},{9,11},{10,... | collective-permute-start | bytes 98312 | tf_op jit(solution)/shard_map/ppermute | solution.py:260
  78.5 4.3 %collective-permute-start.14 = (bf16[2,32,256]{2,1,0:T(8,128)(2,1)S(1)}, bf16[2,32,256]{2,1,0:T(8,128)(2,1)S(1)}, u32[]{:S(2)}, u32[]{:S(2)}) collective-permute-start(bf16[2,32,256]{2,1,0:T(8,128)(2,1)S(1)} %get-tuple-element.41), channel_id=1, source_target_pairs={{0,3},{1,2},{2,1},{3,0},{4,7},{5,6},{6,5},{7,4},{8,11},{9,10},{10,... | collective-permute-start | bytes 98312 | tf_op jit(solution)/shard_map/ppermute | solution.py:260
  79.6 3.2 %collective-permute-start.13 = (bf16[2,32,256]{2,1,0:T(8,128)(2,1)S(1)}, bf16[2,32,256]{2,1,0:T(8,128)(2,1)S(1)}, u32[]{:S(2)}, u32[]{:S(2)}) collective-permute-start(bf16[2,32,256]{2,1,0:T(8,128)(2,1)S(1)} %get-tuple-element.41), channel_id=1, source_target_pairs={{0,1},{1,0},{2,3},{3,2},{4,5},{5,4},{6,7},{7,6},{8,9},{9,8},{10,11... | collective-permute-start | bytes 98312 | tf_op jit(solution)/shard_map/ppermute | solution.py:260
  102.6 4.1 %collective-permute-start.18 = (bf16[32,256]{1,0:T(8,128)(2,1)S(1)}, bf16[32,256]{1,0:T(8,128)(2,1)S(1)}, u32[]{:S(2)}, u32[]{:S(2)}) collective-permute-start(bf16[32,256]{1,0:T(8,128)(2,1)S(1)} %convolution_convert_fusion.2), channel_id=1, source_target_pairs={{0,3},{1,2},{2,1},{3,0},{4,7},{5,6},{6,5},{7,4},{8,11},{9,10},{10,... | collective-permute-start | bytes 49160 | tf_op jit(solution)/shard_map/ppermute | solution.py:286
  104.2 4.4 %collective-permute-start.17 = (bf16[32,256]{1,0:T(8,128)(2,1)S(1)}, bf16[32,256]{1,0:T(8,128)(2,1)S(1)}, u32[]{:S(2)}, u32[]{:S(2)}) collective-permute-start(bf16[32,256]{1,0:T(8,128)(2,1)S(1)} %convolution_convert_fusion.2), channel_id=1, source_target_pairs={{0,2},{1,3},{2,0},{3,1},{4,6},{5,7},{6,4},{7,5},{8,10},{9,11},{10,... | collective-permute-start | bytes 49160 | tf_op jit(solution)/shard_map/ppermute | solution.py:286
  104.7 3.9 %collective-permute-start.16 = (bf16[32,256]{1,0:T(8,128)(2,1)S(1)}, bf16[32,256]{1,0:T(8,128)(2,1)S(1)}, u32[]{:S(2)}, u32[]{:S(2)}) collective-permute-start(bf16[32,256]{1,0:T(8,128)(2,1)S(1)} %convolution_convert_fusion.2), channel_id=1, source_target_pairs={{0,1},{1,0},{2,3},{3,2},{4,5},{5,4},{6,7},{7,6},{8,9},{9,8},{10,11... | collective-permute-start | bytes 49160 | tf_op jit(solution)/shard_map/ppermute | solution.py:286
  126.3 3.8 %collective-permute-start.21 = (bf16[32,256]{1,0:T(8,128)(2,1)S(1)}, bf16[32,256]{1,0:T(8,128)(2,1)S(1)}, u32[]{:S(2)}, u32[]{:S(2)}) collective-permute-start(bf16[32,256]{1,0:T(8,128)(2,1)S(1)} %convolution_convert_fusion.1), channel_id=1, source_target_pairs={{0,3},{1,2},{2,1},{3,0},{4,7},{5,6},{6,5},{7,4},{8,11},{9,10},{10,... | collective-permute-start | bytes 49160 | tf_op jit(solution)/shard_map/ppermute | solution.py:286
  127.3 4.4 %collective-permute-start.20 = (bf16[32,256]{1,0:T(8,128)(2,1)S(1)}, bf16[32,256]{1,0:T(8,128)(2,1)S(1)}, u32[]{:S(2)}, u32[]{:S(2)}) collective-permute-start(bf16[32,256]{1,0:T(8,128)(2,1)S(1)} %convolution_convert_fusion.1), channel_id=1, source_target_pairs={{0,2},{1,3},{2,0},{3,1},{4,6},{5,7},{6,4},{7,5},{8,10},{9,11},{10,... | collective-permute-start | bytes 49160 | tf_op jit(solution)/shard_map/ppermute | solution.py:286
  128.2 3.4 %collective-permute-start.19 = (bf16[32,256]{1,0:T(8,128)(2,1)S(1)}, bf16[32,256]{1,0:T(8,128)(2,1)S(1)}, u32[]{:S(2)}, u32[]{:S(2)}) collective-permute-start(bf16[32,256]{1,0:T(8,128)(2,1)S(1)} %convolution_convert_fusion.1), channel_id=1, source_target_pairs={{0,1},{1,0},{2,3},{3,2},{4,5},{5,4},{6,7},{7,6},{8,9},{9,8},{10,11... | collective-permute-start | bytes 49160 | tf_op jit(solution)/shard_map/ppermute | solution.py:286
  150.3 3.8 %collective-permute-start.24 = (bf16[32,256]{1,0:T(8,128)(2,1)S(1)}, bf16[32,256]{1,0:T(8,128)(2,1)S(1)}, u32[]{:S(2)}, u32[]{:S(2)}) collective-permute-start(bf16[32,256]{1,0:T(8,128)(2,1)S(1)} %convolution_convert_fusion), channel_id=1, source_target_pairs={{0,3},{1,2},{2,1},{3,0},{4,7},{5,6},{6,5},{7,4},{8,11},{9,10},{10,... | collective-permute-start | bytes 49160 | tf_op jit(solution)/shard_map/ppermute | solution.py:286
  151.2 4.1 %collective-permute-start.23 = (bf16[32,256]{1,0:T(8,128)(2,1)S(1)}, bf16[32,256]{1,0:T(8,128)(2,1)S(1)}, u32[]{:S(2)}, u32[]{:S(2)}) collective-permute-start(bf16[32,256]{1,0:T(8,128)(2,1)S(1)} %convolution_convert_fusion), channel_id=1, source_target_pairs={{0,2},{1,3},{2,0},{3,1},{4,6},{5,7},{6,4},{7,5},{8,10},{9,11},{10,... | collective-permute-start | bytes 49160 | tf_op jit(solution)/shard_map/ppermute | solution.py:286
  152.2 3.1 %collective-permute-start.22 = (bf16[32,256]{1,0:T(8,128)(2,1)S(1)}, bf16[32,256]{1,0:T(8,128)(2,1)S(1)}, u32[]{:S(2)}, u32[]{:S(2)}) collective-permute-start(bf16[32,256]{1,0:T(8,128)(2,1)S(1)} %convolution_convert_fusion), channel_id=1, source_target_pairs={{0,1},{1,0},{2,3},{3,2},{4,5},{5,4},{6,7},{7,6},{8,9},{9,8},{10,11... | collective-permute-start | bytes 49160 | tf_op jit(solution)/shard_map/ppermute | solution.py:286
  155.3 18.4 %collective-permute-start.25 = (bf16[2,32,256]{2,1,0:T(8,128)(2,1)S(1)}, bf16[2,32,256]{2,1,0:T(8,128)(2,1)S(1)}, u32[]{:S(2)}, u32[]{:S(2)}) collective-permute-start(bf16[2,32,256]{2,1,0:T(8,128)(2,1)S(1)} %pad_maximum_fusion.6), channel_id=1, source_target_pairs={{0,4},{4,0},{1,5},{5,1},{2,6},{6,2},{3,7},{7,3},{8,12},{12,8},{9,1... | collective-permute-start | bytes 98312 | tf_op jit(solution)/shard_map/ppermute | solution.py:24
